TPU v7x, 32 devices: a whole 2x2x4 slice. The times are simulated.
32 devices in a mesh: segment: 8 (over z, x), dp: 4 (over y, core).
Axes of the slice: x: 2, y: 2, z: 4, core: 2. Of those that a mesh axis runs over, the one named last changes fastest.
Arguments:
- checkpoint: bfloat16 [8, 2, 4, 16, 16, 1024], P('segment', None, 'dp'), may hold values from -6 to 6
- cotangent: bfloat16 [2, 4, 16, 16, 1024], P(None, 'dp'), may hold values from -6 to 6
- depthwise: float32 [8, 2, 25, 1024], P('segment'), may hold values from -1.8 to 1.8
- pointwise: bfloat16 [8, 1024, 2, 1024], P('segment', 'dp'), may hold values from -0.1875 to 0.1875
- genotype: int32 [8], P('segment'), may hold values from 0 to 2, as said below
Outputs:
- grad_input: bfloat16 [8, 2, 4, 16, 16, 1024], P('segment', None, 'dp')
- grad_point: float32 [8, 1024, 2, 1024], P('segment', 'dp')
- grad_depth: float32 [8, 2, 25, 1024], P('segment')
Inputs may be any that keep to these rules, and one draw needn't show every extreme that they name: `genotype`: 0 separable 3x3, 1 separable 5x5, 2 dilated separable 3x3; both 0 and 2 occur.
All inputs are finite; a program needn't handle non-finite values.
Results may differ from a plain program's by a relative error of at most 0.025.
Values may be sent and summed in bfloat16 or wider, within the bound.
No kernel may reach another device: no remote copies, remote signals or barrier semaphores. Data moves between devices by JAX's collectives and lax.ppermute only.
A program may use at most 128 MiB of HBM per device.

v0:
```python
import functools

import jax
import jax.numpy as jnp
from jax import lax
from jax.experimental import pallas as pl
from jax.experimental.pallas import tpu as pltpu
from jax.sharding import PartitionSpec as P

LANES = 128
TAPS = 25
KEPT = (
    [(r, c) for r in (-1, 0, 1) for c in (-1, 0, 1)],
    [(r, c) for r in (-2, -1, 0, 1, 2) for c in (-2, -1, 0, 1, 2)],
    [(r, c) for r in (-2, 0, 2) for c in (-2, 0, 2)],
)
MIB = 2**20


def moved(value, step):
    if step == 0:
        return value
    side = value.shape[0]
    place = lax.broadcasted_iota(jnp.int32, value.shape, 0) + step
    return jnp.where((place >= 0) & (place < side), pltpu.roll(value, (-step) % side, 0), 0.0)


def conv(source, taps, kind, emit):
    side = source.shape[1]

    def run(kept):
        cols = sorted({c for _, c in kept})
        lines = sorted({r for r, _ in kept})

        def lane(chunk, carry):
            lanes = pl.ds(pl.multiple_of(chunk * LANES, LANES), LANES)
            weight = {(r, c): taps(5 * (r + 2) + c + 2, lanes) for r, c in kept}

            def row(p, carry):
                near = {r: source[p + r + 2, :, lanes] for r in lines}
                total = None
                for c in cols:
                    column = None
                    for r in lines:
                        term = weight[r, c] * near[r]
                        column = term if column is None else column + term
                    column = moved(column, c)
                    total = column if total is None else total + column
                emit(pl.ds(pl.multiple_of(p * side, side), side), lanes, total)
                return carry

            lax.fori_loop(0, side, row, 0, unroll=16)
            return carry

        lax.fori_loop(0, source.shape[2] // LANES, lane, 0)

    for which in range(3):
        pl.when(kind == which)(functools.partial(run, KEPT[which]))


def clear_edges(source):
    side = source.shape[1]
    zero = jnp.zeros((2,) + source.shape[1:], jnp.float32)
    source[:2] = zero
    source[side + 2 :] = zero


def chain_kernel(scalars, *refs, pair, visits, parts, aliased, side):
    up_in = refs[0]
    xs, slopes, ks = refs[1:3], refs[3:5], refs[5:7]
    blocks = (refs[7 : 7 + parts], refs[7 + parts : 7 + 2 * parts])
    at = 7 + 2 * parts + aliased
    held = 4 if visits[0] else 5
    outs = [refs[at + 2 * i : at + 2 * i + 2] for i in range(held)]
    in_out, pre_out, mix_out, lin_out = outs[:4]
    leave = refs[at + 2 * held]
    panels, factor, k_at, left_at, flat_at, source, came, went = refs[at + 2 * held + 1 :]
    width = panels.shape[1] // parts
    steps = 2 * len(visits)

    def piece(step, part):
        return panels.at[step, pl.ds(part * width, width)], came.at[step * (parts + 1) + part]

    def other(step):
        return factor.at[step], came.at[step * (parts + 1) + parts]

    def taps_of(visit):
        return k_at.at[visit], came.at[steps * (parts + 1) + visit]

    def fetch(step, order):
        slot = order[visits[step // 2]]
        stage = step % 2
        for part in range(parts):
            place, sem = piece(step, part)
            pltpu.make_async_copy(blocks[slot][part].at[1 - stage], place, sem).start()
        if stage == 0:
            place, sem = taps_of(step // 2)
            pltpu.make_async_copy(ks[slot], place, sem).start()
        place, sem = other(step)
        pltpu.make_async_copy((xs if stage else slopes)[slot], place, sem).start()

    def fetch_for(step):
        pl.when(scalars[3] == 1)(functools.partial(fetch, step, (0, 1)))
        pl.when(scalars[3] == 0)(functools.partial(fetch, step, (1, 0)))

    def send(value, outs, slot, sem):
        for which in range(2):
            pl.when(slot == which)(pltpu.make_async_copy(value, outs[which], went.at[sem]).start)

    def wait(place, sem):
        pltpu.make_async_copy(place, place, sem).wait()

    def go():
        first = pltpu.make_async_copy(up_in, left_at.at[0], came.at[steps * (parts + 1) + len(visits)])
        first.start()
        fetch_for(0)
        clear_edges(source)
        first.wait()

        def one(step, carry):
            index = step // 2
            stage = step % 2
            slot = (visits[0] + index) ^ (1 - scalars[3])
            left = left_at.at[step]
            for later in range(1, steps):
                pl.when(step == later - 1)(functools.partial(fetch_for, later))

            def multiply(part, carry):
                place, sem = piece(step, part)
                wait(place, sem)
                flat = lax.dot_general(
                    left[...], place[...], (((1,), (1,)), ((), ())), preferred_element_type=jnp.float32
                )
                wide = pl.ds(pl.multiple_of((scalars[0] ^ part) * width, LANES), width)
                flat_at[step, :, wide] = flat.astype(jnp.bfloat16)
                source[2 : side + 2, :, wide] = flat.reshape(side, side, width)
                return carry

            lax.fori_loop(0, parts, multiply, 0)

            @pl.when(stage == 0)
            def _():
                wait(*taps_of(index))
                if visits[0] == 0:
                    send(left, outs[4], slot, 3 * step)
                send(flat_at.at[step], mix_out, slot, 3 * step + 1)

            @pl.when(stage == 1)
            def _():
                send(flat_at.at[step], lin_out, slot, 3 * step + 1)

            wait(*other(step))
            result = left_at.at[step + 1]

            def taps(tap, lanes):
                return k_at[index, 1 - stage, TAPS - 1 - tap, lanes][None]

            def scaled(rows, lanes, total):
                slope = factor[step, rows, lanes].astype(jnp.float32)
                result[rows, lanes] = (total * slope).astype(jnp.bfloat16)

            def gated(rows, lanes, total):
                total = jnp.where(factor[step, rows, lanes].astype(jnp.float32) > 0, total, 0.0)
                base = left_at[2 * index, rows, lanes].astype(jnp.float32)
                result[rows, lanes] = (base + total).astype(jnp.bfloat16)

            for which, emit in enumerate((scaled, gated)):
                pl.when(stage == which)(functools.partial(conv, source, taps, scalars[1 + slot], emit))

            @pl.when(stage == 0)
            def _():
                send(result, pre_out, slot, 3 * step + 2)

            @pl.when(stage == 1)
            def _():
                send(result, in_out, slot, 3 * step + 2)
                if len(visits) == 1 and visits[0] == 0:
                    send(result, outs[4], 1 - slot, 3 * step)

            return carry

        lax.fori_loop(0, steps, one, 0)
        last = pltpu.make_async_copy(left_at.at[steps], leave, came.at[0])
        last.start()
        for step in range(steps):
            for which in range(3):
                if which > 0 or (step % 2 == 0 and visits[0] == 0) or visits == (0,):
                    wait(flat_at.at[0], went.at[3 * step + which])
        last.wait()

    pl.when(scalars[4] == pair)(go)


def chain(scalars, up, xs, slopes, ks, blocks, state, pair, visits, side):
    parts = len(blocks[0])
    rows, channels = up.shape
    steps = 2 * len(visits)
    flat = jax.ShapeDtypeStruct((rows, channels), jnp.bfloat16)
    anywhere = pl.BlockSpec(memory_space=pl.ANY)
    inputs = [up, *xs, *slopes, *ks, *blocks[0], *blocks[1], *state]
    first_state = 1 + len(inputs) - len(state)
    count = 8 if visits[0] else 10
    outs = pl.pallas_call(
        functools.partial(chain_kernel, pair=pair, visits=visits, parts=parts, aliased=len(state), side=side),
        in_specs=[pl.BlockSpec(memory_space=pltpu.SMEM)] + [anywhere] * len(inputs),
        out_specs=[anywhere] * (count + 1),
        out_shape=[flat] * (count + 1),
        input_output_aliases={first_state + i: i for i in range(len(state))},
        scratch_shapes=[
            pltpu.VMEM((steps, channels, channels), jnp.bfloat16),
            pltpu.VMEM((steps, rows, channels), jnp.bfloat16),
            pltpu.VMEM((len(visits),) + ks[0].shape, jnp.float32),
            pltpu.VMEM((steps + 1, rows, channels), jnp.bfloat16),
            pltpu.VMEM((steps, rows, channels), jnp.bfloat16),
            pltpu.VMEM((side + 4, side, channels), jnp.float32),
            pltpu.SemaphoreType.DMA((steps * (parts + 1) + len(visits) + 1,)),
            pltpu.SemaphoreType.DMA((3 * steps,)),
        ],
        compiler_params=pltpu.CompilerParams(vmem_limit_bytes=58 * MIB),
        cost_estimate=pl.CostEstimate(flops=10**10, bytes_accessed=12 * MIB, transcendentals=0),
    )(scalars, *inputs)
    return tuple(outs[:count]), outs[count]


def start_kernel(scalars, x, k, start, source, *, slot, side):
    clear_edges(source)
    source[2 : side + 2] = jnp.maximum(x[...].astype(jnp.float32), 0.0).reshape(side, side, x.shape[1])

    def emit(rows, lanes, total):
        start[rows, lanes] = total.astype(jnp.bfloat16)

    conv(source, lambda tap, lanes: k[0, tap, lanes][None], scalars[1 + slot], emit)


def rest_kernel(scalars, start, *refs, slot, side, parts, mixes):
    if mixes:
        k, *refs = refs
    blocks = refs[:parts]
    panel, came = refs[-2:]
    hidden, slope = refs[parts : parts + 2]
    width = blocks[0].shape[1]
    copies = [pltpu.make_async_copy(blocks[part].at[0], panel.at[part], came.at[part]) for part in range(parts)]
    for copy in copies:
        copy.start()
    if mixes:
        mixed, source = refs[parts + 2 : parts + 4]
        clear_edges(source)
    for copy in copies:
        copy.wait()

    def columns(part, carry):
        wide = pl.ds(pl.multiple_of(part * width, LANES), width)
        flat = None
        for inner in range(parts):
            below = pl.ds(pl.multiple_of((scalars[0] ^ inner) * width, LANES), width)
            term = jnp.dot(start[:, below], panel[inner, :, wide], preferred_element_type=jnp.float32)
            flat = term if flat is None else flat + term
        sigma = jax.nn.sigmoid(flat)
        rounded = (flat * sigma).astype(jnp.bfloat16)
        hidden[:, wide] = rounded
        slope[:, wide] = (sigma * (1.0 + flat * (1.0 - sigma))).astype(jnp.bfloat16)
        if mixes:
            source[2 : side + 2, :, wide] = rounded.astype(jnp.float32).reshape(side, side, width)
        return carry

    lax.fori_loop(0, parts, columns, 0)
    if mixes:

        def emit(rows, lanes, total):
            mixed[rows, lanes] = total.astype(jnp.bfloat16)

        conv(source, lambda tap, lanes: k[1, tap, lanes][None], scalars[1 + slot], emit)


SMEM = pl.BlockSpec(memory_space=pltpu.SMEM)
VMEM = pl.BlockSpec(memory_space=pltpu.VMEM)


def forward_start(scalars, x, k, slot, side):
    rows, channels = x.shape
    return pl.pallas_call(
        functools.partial(start_kernel, slot=slot, side=side),
        in_specs=[SMEM, VMEM, VMEM],
        out_specs=VMEM,
        out_shape=jax.ShapeDtypeStruct((rows, channels), jnp.bfloat16),
        scratch_shapes=[pltpu.VMEM((side + 4, side, channels), jnp.float32)],
        compiler_params=pltpu.CompilerParams(vmem_limit_bytes=58 * MIB),
        cost_estimate=pl.CostEstimate(flops=1, bytes_accessed=1, transcendentals=0),
    )(scalars, x, k)


def forward_rest(scalars, start, k, blocks, slot, side, mixes):
    parts = len(blocks)
    rows, channels = start.shape
    outs = 3 if mixes else 2
    return pl.pallas_call(
        functools.partial(rest_kernel, slot=slot, side=side, parts=parts, mixes=mixes),
        in_specs=[SMEM, VMEM] + [VMEM] * mixes + [pl.BlockSpec(memory_space=pl.ANY)] * parts,
        out_specs=[VMEM] * outs,
        out_shape=[jax.ShapeDtypeStruct((rows, channels), jnp.bfloat16)] * outs,
        scratch_shapes=([pltpu.VMEM((side + 4, side, channels), jnp.float32)] if mixes else [])
        + [pltpu.VMEM((parts, channels // parts, channels), jnp.bfloat16), pltpu.SemaphoreType.DMA((parts,))],
        compiler_params=pltpu.CompilerParams(vmem_limit_bytes=58 * MIB),
        cost_estimate=pl.CostEstimate(flops=1, bytes_accessed=1, transcendentals=0),
    )(scalars, start, *([k] if mixes else []), *blocks)


def taps_kernel(scalars, x, lin, hidden, mix, out, source, *, slot, side):
    channels = x.shape[1]
    clear_edges(source)
    out[...] = jnp.zeros_like(out)

    def run(kept):
        cols = sorted({c for _, c in kept})
        lines = sorted({r for r, _ in kept})
        for which, (value, grad) in enumerate(((x, lin), (hidden, mix))):

            def lane(chunk, carry):
                lanes = pl.ds(pl.multiple_of(chunk * LANES, LANES), LANES)
                flat = value[:, lanes].astype(jnp.float32)
                if which == 0:
                    flat = jnp.maximum(flat, 0.0)
                source[2 : side + 2] = flat.reshape(side, side, LANES)

                def row(p, sums):
                    rows = pl.ds(pl.multiple_of(p * side, side), side)
                    here = grad[rows, lanes].astype(jnp.float32)
                    shifted = {c: moved(here, -c) for c in cols}
                    near = {r: source[p + r + 2] for r in lines}
                    new = []
                    for old, (r, c) in zip(sums, kept):
                        term = near[r] * shifted[c]
                        new.append(old + (term[: side // 2] + term[side // 2 :]))
                    return tuple(new)

                blank = jnp.zeros((side // 2, LANES), jnp.float32)
                sums = lax.fori_loop(0, side, row, (blank,) * len(kept), unroll=4)
                for total, (r, c) in zip(sums, kept):
                    out[which, 5 * (r + 2) + c + 2, lanes] = jnp.sum(total, axis=0)
                return carry

            lax.fori_loop(0, channels // LANES, lane, 0)

    for kind in range(3):
        pl.when(scalars[1 + slot] == kind)(functools.partial(run, KEPT[kind]))


def tap_sums(scalars, x, lin, hidden, mix, slot, side):
    channels = x.shape[1]
    return pl.pallas_call(
        functools.partial(taps_kernel, slot=slot, side=side),
        in_specs=[SMEM] + [VMEM] * 4,
        out_specs=VMEM,
        out_shape=jax.ShapeDtypeStruct((2, TAPS, channels), jnp.float32),
        scratch_shapes=[pltpu.VMEM((side + 4, side, LANES), jnp.float32)],
        compiler_params=pltpu.CompilerParams(vmem_limit_bytes=58 * MIB),
        cost_estimate=pl.CostEstimate(flops=1, bytes_accessed=1, transcendentals=0),
    )(scalars, x, lin, hidden, mix)


def joined_kernel(first, first_came, second, second_came, out, *, scale):
    out[:, 0, :] = (first[...] + first_came[...].astype(jnp.float32)) * scale
    out[:, 1, :] = (second[...] + second_came[...].astype(jnp.float32)) * scale


def joined(first, first_came, second, second_came, scale):
    share, channels = first.shape
    return pl.pallas_call(
        functools.partial(joined_kernel, scale=scale),
        in_specs=[VMEM] * 4,
        out_specs=VMEM,
        out_shape=jax.ShapeDtypeStruct((share, 2, channels), jnp.float32),
        compiler_params=pltpu.CompilerParams(vmem_limit_bytes=24 * MIB),
        cost_estimate=pl.CostEstimate(flops=1, bytes_accessed=1, transcendentals=0),
    )(first, first_came, second, second_came)


def swap(value, axis, bit):
    count = lax.axis_size(axis)
    return lax.ppermute(value, axis, [(source, source ^ bit) for source in range(count)])


def inner_rows(left, right):
    return lax.dot_general(left, right, (((0,), (0,)), ((), ())), preferred_element_type=jnp.float32)


def products(lefts, right_own, right_other):
    leave = inner_rows(lefts[0], right_own) + inner_rows(lefts[1], right_other)
    return leave.astype(jnp.bfloat16), inner_rows(lefts[2], right_own) + inner_rows(lefts[3], right_other)


def doubled(held, bits):
    for bit in bits:
        held = held + [(mask ^ bit, swap(part, "dp", bit)) for mask, part in held]
    return held


def panel_blocks(held, data, dp, width):
    held = doubled(held, [1])
    held = [part for _, part in sorted(held, key=lambda pair: pair[0])]
    share, channels = held[0].shape[1:]
    if share == width:
        return held, data
    panel = jnp.zeros((2, channels, channels), held[0].dtype)
    for mask, part in enumerate(held):
        panel = lax.dynamic_update_slice(panel, part, (0, (data ^ mask) * share, 0))
    return [panel[:, at : at + width] for at in range(0, channels, width)], jnp.zeros_like(data)


def body(checkpoint, cotangent, depthwise, pointwise, genotype):
    micro, images, side = checkpoint.shape[1:4]
    channels = checkpoint.shape[5]
    rows = images * side * side
    dp = lax.axis_size("dp")
    sections = lax.axis_size("segment")
    pairs = sections // 2
    segment = lax.axis_index("segment")
    data = lax.axis_index("dp")
    half = segment % 2
    pair = segment // 2
    is_high = half == 1
    share = channels // dp
    width = 256
    mean_scale = 1.0 / (micro * images * dp)

    x_all = checkpoint[0].reshape(micro, rows, channels)
    x_own = lax.dynamic_index_in_dim(x_all, half, 0, keepdims=False)
    x_other = lax.dynamic_index_in_dim(x_all, 1 - half, 0, keepdims=False)
    kind_row = jnp.full((2, 1, channels), genotype[0].astype(jnp.float32))
    k_own = jnp.concatenate([depthwise[0], kind_row], axis=1)

    far_bits = [1 << bit for bit in range(dp.bit_length() - 2, 0, -1)]
    own_rows = jnp.swapaxes(pointwise[0], 0, 1)
    own_held = doubled([(0, own_rows)], far_bits)
    partner_rows, x_sent, k_sent = lax.optimization_barrier((swap(own_rows, "segment", 1), x_other, k_own))
    x_partner = swap(x_sent, "segment", 1)
    k_partner = swap(k_sent, "segment", 1)
    partner_held = doubled([(0, partner_rows)], far_bits)
    own_blocks, turned = panel_blocks(own_held, data, dp, width)
    scalars_own = jnp.stack([turned, genotype[0], genotype[0], half, pair]).astype(jnp.int32)
    first_own = forward_start(scalars_own, x_own, k_own, 0, side)
    hidden_own, slope_own, mixed_own = forward_rest(scalars_own, first_own, k_own, own_blocks, 0, side, True)
    upstream = lax.dynamic_index_in_dim(cotangent, half, 0, keepdims=False).reshape(rows, channels)
    x_partner, k_partner, slope_own, upstream = lax.optimization_barrier(
        (x_partner, k_partner, slope_own, upstream)
    )
    kind_partner = k_partner[0, TAPS, 0].astype(jnp.int32)
    scalars = jnp.stack([turned, genotype[0], kind_partner, half, pair]).astype(jnp.int32)
    first_partner = forward_start(scalars, x_partner, k_partner, 1, side)
    far, first_partner = lax.optimization_barrier(([part for _, part in partner_held], first_partner))
    partner_held = [(mask, part) for (mask, _), part in zip(partner_held, far)]
    partner_blocks, _ = panel_blocks(partner_held, data, dp, width)
    blocks = (own_blocks, partner_blocks)
    hidden_partner, slope_partner = forward_rest(
        scalars, first_partner, k_partner, partner_blocks, 1, side, False
    )

    xs, slopes, ks = (x_own, x_partner), (slope_own, slope_partner), (k_own, k_partner)
    state = ()

    def rows_of(left, core):
        return jnp.concatenate(
            [lax.dynamic_slice(left, (0, (2 * at + core) * share), (rows, share)) for at in range(dp // 2)],
            axis=1,
        )

    for turn in range(pairs):
        source = pairs - 1 - turn
        if turn < pairs - 1:
            state, leaving = chain(scalars, upstream, xs, slopes, ks, blocks, state, source, (0, 1), side)
            upstream = lax.ppermute(
                leaving, "segment", [(2 * source + h, 2 * source - 2 + h) for h in range(2)]
            )
            if turn == 0:
                x_late, state = lax.optimization_barrier((x_other, state))
                first_other = forward_start(scalars_own, x_late, k_own, 0, side)
                _, _, mixed_other = forward_rest(
                    scalars_own, first_other, k_own, own_blocks, 0, side, True
                )
                state, first_other, mixed_other = lax.optimization_barrier((state, first_other, mixed_other))
            if turn == min(1, pairs - 2):
                first_lefts, second_lefts = (
                    [rows_of(left, core) for core in (1 - data % 2, data % 2) for left in pair_of]
                    for pair_of in ((first_own, first_other), (mixed_own, mixed_other))
                )
                state, first_lefts, second_lefts = lax.optimization_barrier((state, first_lefts, second_lefts))
        else:
            state, leaving = chain(scalars, upstream, xs, slopes, ks, blocks, state, source, (0,), side)
            up_own, up_partner = state[8:]
            up_other = swap(up_partner, "segment", 1)
            state, _ = chain(scalars, leaving, xs, slopes, ks, blocks, state[:8], source, (1,), side)

    in_own, in_partner, pre_own, pre_partner, mix_own, mix_partner, lin_own, lin_partner = state
    def halved(total, came, bit):
        def part(index):
            def pick(value):
                value = value.reshape(value.shape[:-2] + (2, -1, channels))
                return lax.dynamic_index_in_dim(value, index, value.ndim - 3, keepdims=False)

            return pick(total) + pick(came).astype(jnp.float32)

        mine = (data // bit) % 2
        return part(mine), part(1 - mine).astype(jnp.bfloat16)

    def scattered(stay, leave):
        bit = dp // 2
        while bit > 2:
            came = swap(leave, "dp", bit)
            bit //= 2
            stay, leave = halved(stay, came, bit)
        return stay.reshape(share, channels), swap(leave, "dp", bit).reshape(share, channels)

    pre_other = swap(pre_partner, "segment", 1)
    leave, stay = products(second_lefts, up_own, up_other)
    stay, leave = halved(stay, swap(leave, "dp", 1), dp // 2)
    second = scattered(stay, leave)
    pre_other, in_partner = lax.optimization_barrier((pre_other, in_partner))
    in_other = swap(in_partner, "segment", 1)
    leave, stay = products(first_lefts, pre_own, pre_other)
    stay, leave = halved(stay, swap(leave, "dp", 1), dp // 2)
    lin_partner, leave = lax.optimization_barrier((lin_partner, leave))
    first = scattered(stay, leave)
    sums_partner = tap_sums(scalars, x_partner, lin_partner, hidden_partner, mix_partner, 1, side)
    grad_input = jnp.where(is_high, jnp.stack([in_other, in_own]), jnp.stack([in_own, in_other]))
    lin_own, second, grad_input = lax.optimization_barrier((lin_own, second, grad_input))
    sums_own = tap_sums(scalars, x_own, lin_own, hidden_own, mix_own, 0, side)

    total = sums_own + swap(sums_partner.astype(jnp.bfloat16), "segment", 1).astype(jnp.float32)
    bit = 1
    while bit < dp:
        sent = total.astype(jnp.bfloat16)
        total = sent.astype(jnp.float32) + swap(sent, "dp", bit).astype(jnp.float32)
        bit *= 2
    grad_depth = total * mean_scale
    grad_point = joined(*first, *second, mean_scale)

    return (
        grad_input.reshape(checkpoint.shape),
        grad_point[None],
        grad_depth[None],
    )


def solution(mesh):
    placed = (
        P("segment", None, "dp", None, None, None),
        P(None, "dp", None, None, None),
        P("segment", None, None, None),
        P("segment", "dp", None, None),
        P("segment"),
    )
    return jax.shard_map(
        body,
        mesh=mesh,
        in_specs=placed,
        out_specs=(
            P("segment", None, "dp", None, None, None),
            P("segment", "dp", None, None),
            P("segment", None, None, None),
        ),
        check_vma=False,
    )
```

profile of v0, /device:TPU:0, one launch (start us, length us, event | category | flops | bytes accessed | tf_op | source)
XLA Modules:
  0.0 229.2 jit_solution(15826724909022200901)
XLA Ops:
  0.7 1.6 copy.52
  2.3 3.0 %collective-permute-start.4 = (bf16[2,256,1024]{2,1,0:T(8,128)(2,1)S(1)}, bf16[2,256,1024]{2,1,0:T(8,128)(2,1)S(1)}, u32[]{:S(2)}, u32[]{:S(2)}) collective-permute-start(bf16[2,256,1024]{2,1,0:T(8,128)(2,1)S(1)} %bitcast.55), channel_id=1, source_target_pairs={{0,2},{1,3},{2,0},{3,1},{4,6},{5,7},{6,4},{7,5},{8,10},{9,11},{10,... | collective-permute-start | bytes 3145736 | tf_op jit(solution)/shard_map/ppermute | solution.py:380
  5.3 1.5 collective-permute-start
  6.8 21.7 %collective-permute-done.4.refs_3_.refs_9_ = bf16[2,256,1024]{2,1,0:T(8,128)(2,1)S(1)} collective-permute-done((bf16[2,256,1024]{2,1,0:T(8,128)(2,1)S(1)}, bf16[2,256,1024]{2,1,0:T(8,128)(2,1)S(1)}, u32[]{:S(2)}, u32[]{:S(2)}) %collective-permute-start.4) | collective-permute-done | bytes 1048608 | tf_op jit(solution)/shard_map/ppermute | solution.py:380
  28.5 2.7 %dynamic-slice_bitcast_fusion = (bf16[256,1024]{1,0:T(8,128)(2,1)}, bf16[256,1024]{1,0:T(8,128)(2,1)}) fusion(bf16[2,256,1024]{2,1,0:T(8,128)(2,1)} %bitcast.72, s32[]{:T(128)S(6)} %select_n.88, s32[]{:T(128)S(6)} %select_n.86), kind=kLoop, calls=%fused_computation.12 | loop fusion | bytes 2097160 | tf_op jit(solution)/shard_map/jit(dynamic_index_in_dim)/squeeze | solution.py:427
  31.9 1.8 collective-permute-start.6
  33.7 1.5 collective-permute-start.1
  36.4 4.1 %shard_map.76.start = bf16[256,1024]{1,0:T(8,128)(2,1)} custom-call(s32[5]{0:T(128)} %stack.38.scalars, bf16[256,1024]{1,0:T(8,128)(2,1)} %get-tuple-element.244.x.refs_1_, f32[2,26,1024]{2,1,0:T(8,128)} %copy-done.2), custom_call_target="tpu_custom_call" | custom-call | flops 1 | bytes 1 | tf_op jit(solution)/shard_map/pallas_call | solution.py:281
  41.4 7.5 %shard_map.77 = (bf16[256,1024]{1,0:T(8,128)(2,1)}, bf16[256,1024]{1,0:T(8,128)(2,1)}, bf16[256,1024]{1,0:T(8,128)(2,1)}) custom-call(s32[5]{0:T(128)} %stack.38.scalars, bf16[256,1024]{1,0:T(8,128)(2,1)} %shard_map.76.start, f32[2,26,1024]{2,1,0:T(8,128)} %copy-done.2, bf16[2,256,1024]{2,1,0:T(8,128)(2,1)} %bitcast.58, ...), custom_call_target="tpu_custom_call" | custom-call | flops 1 | bytes 1 | tf_op jit(solution)/shard_map/pallas_call | solution.py:296
  48.9 4.5 %collective-permute-done.2.k.refs_6_ = f32[2,26,1024]{2,1,0:T(8,128)} collective-permute-done((f32[2,26,1024]{2,1,0:T(8,128)S(1)}, f32[2,26,1024]{2,1,0:T(8,128)}, u32[]{:S(2)}, u32[]{:S(2)}) %collective-permute-start.2) | collective-permute-done | bytes 213024 | tf_op jit(solution)/shard_map/ppermute | solution.py:380
  53.3 1.3 slice.3
  56.0 2.9 %shard_map.78.start = bf16[256,1024]{1,0:T(8,128)(2,1)} custom-call(s32[5]{0:T(128)} %stack.40.scalars, bf16[256,1024]{1,0:T(8,128)(2,1)} %collective-permute-done.1.x.refs_2_, f32[2,26,1024]{2,1,0:T(8,128)} %collective-permute-done.2.k.refs_6_), custom_call_target="tpu_custom_call" | custom-call | flops 1 | bytes 1 | tf_op jit(solution)/shard_map/pallas_call | solution.py:281
  59.3 2.4 %collective-permute-done.7.refs_1_.refs_12_ = bf16[2,256,1024]{2,1,0:T(8,128)(2,1)S(1)} collective-permute-done((bf16[2,256,1024]{2,1,0:T(8,128)(2,1)}, bf16[2,256,1024]{2,1,0:T(8,128)(2,1)S(1)}, u32[]{:S(2)}, u32[]{:S(2)}) %collective-permute-start.7) | collective-permute-done | bytes 1048608 | tf_op jit(solution)/shard_map/ppermute | solution.py:380
  61.7 1.5 collective-permute-done.8.refs_3_.refs_14_
  64.2 5.0 %shard_map.79 = (bf16[256,1024]{1,0:T(8,128)(2,1)}, bf16[256,1024]{1,0:T(8,128)(2,1)}) custom-call(s32[5]{0:T(128)} %stack.40.scalars, bf16[256,1024]{1,0:T(8,128)(2,1)} %shard_map.78.start, bf16[2,256,1024]{2,1,0:T(8,128)(2,1)} %collective-permute-done.refs_0_.refs_11_, bf16[2,256,1024]{2,1,0:T(8,128)(2,1)} %copy-done.8, ...), custom_call_target="tpu_custom_call" | custom-call | flops 1 | bytes 1 | tf_op jit(solution)/shard_map/pallas_call | solution.py:296
  70.4 1.6 collective-permute-start.9
  72.2 4.1 %shard_map.81.start = bf16[256,1024]{1,0:T(8,128)(2,1)} custom-call(s32[5]{0:T(128)} %stack.38.scalars, bf16[256,1024]{1,0:T(8,128)(2,1)} %get-tuple-element.153.x, f32[2,26,1024]{2,1,0:T(8,128)} %copy-done.2), custom_call_target="tpu_custom_call" | custom-call | flops 1 | bytes 1 | tf_op jit(solution)/shard_map/pallas_call | solution.py:281
  76.4 7.4 %shard_map.82 = (bf16[256,1024]{1,0:T(8,128)(2,1)}, bf16[256,1024]{1,0:T(8,128)(2,1)}, bf16[256,1024]{1,0:T(8,128)(2,1)}) custom-call(s32[5]{0:T(128)} %stack.38.scalars, bf16[256,1024]{1,0:T(8,128)(2,1)} %shard_map.81.start, f32[2,26,1024]{2,1,0:T(8,128)} %copy-done.2, bf16[2,256,1024]{2,1,0:T(8,128)(2,1)} %bitcast.60, ...), custom_call_target="tpu_custom_call" | custom-call | flops 1 | bytes 1 | tf_op jit(solution)/shard_map/pallas_call | solution.py:296
  83.8 1.2 shard_map.83
  87.8 1.3 collective-permute-start.11
  89.1 71.7 %collective-permute-done.11.refs_0_ = bf16[256,1024]{1,0:T(8,128)(2,1)} collective-permute-done((bf16[256,1024]{1,0:T(8,128)(2,1)}, bf16[256,1024]{1,0:T(8,128)(2,1)}, u32[]{:S(2)}, u32[]{:S(2)}) %collective-permute-start.11) | collective-permute-done | bytes 524320 | tf_op jit(solution)/shard_map/ppermute | solution.py:471
  160.8 8.1 %shard_map.85 = (bf16[256,1024]{1,0:T(8,128)(2,1)}, bf16[256,1024]{1,0:T(8,128)(2,1)}, bf16[256,1024]{1,0:T(8,128)(2,1)}, bf16[256,1024]{1,0:T(8,128)(2,1)}, bf1...) custom-call(s32[5]{0:T(128)} %stack.40.scalars, ...), custom_call_target="tpu_custom_call", output_to_operand_aliasing={{0}: (16, {}), {1}: (17, {}), {2}: (18, {}), {3}: (19, {}),... | custom-call | flops 10000000000 | bytes 12582912 | tf_op jit(solution)/shard_map/pallas_call | solution.py:203
  168.9 2.8 %collective-permute-start.12 = (bf16[256,1024]{1,0:T(8,128)(2,1)}, bf16[256,1024]{1,0:T(8,128)(2,1)S(1)}, u32[]{:S(2)}, u32[]{:S(2)}) collective-permute-start(bf16[256,1024]{1,0:T(8,128)(2,1)} %get-tuple-element.213), channel_id=1, source_target_pairs={{0,4},{4,0},{8,12},{12,8},{16,20},{20,16},{24,28},{28,24},{1,5},{5... | collective-permute-start | bytes 1572872 | tf_op jit(solution)/shard_map/ppermute | solution.py:380
  171.7 10.3 %shard_map.86 = (bf16[256,1024]{1,0:T(8,128)(2,1)}, bf16[256,1024]{1,0:T(8,128)(2,1)}, bf16[256,1024]{1,0:T(8,128)(2,1)}, bf16[256,1024]{1,0:T(8,128)(2,1)}, bf1...) custom-call(s32[5]{0:T(128)} %stack.40.scalars, ...), custom_call_target="tpu_custom_call", output_to_operand_aliasing={{0}: (16, {}), {1}: (17, {}), {2}: (18, {}), {3}: (19, {}),... | custom-call | flops 10000000000 | bytes 12582912 | tf_op jit(solution)/shard_map/pallas_call | solution.py:203
  183.6 10.6 %collective-permute-done.15 = bf16[256,1024]{1,0:T(8,128)(2,1)S(1)} collective-permute-done((bf16[256,1024]{1,0:T(8,128)(2,1)}, bf16[256,1024]{1,0:T(8,128)(2,1)S(1)}, u32[]{:S(2)}, u32[]{:S(2)}) %collective-permute-start.15) | collective-permute-done | bytes 524320 | tf_op jit(solution)/shard_map/ppermute | solution.py:380
  199.3 4.9 %shard_map.89 = f32[2,25,1024]{2,1,0:T(8,128)} custom-call(s32[5]{0:T(128)} %stack.40.scalars, bf16[256,1024]{1,0:T(8,128)(2,1)} %collective-permute-done.1.x.refs_2_, bf16[256,1024]{1,0:T(8,128)(2,1)} %get-tuple-element.234.lin, bf16[256,1024]{1,0:T(8,128)(2,1)} %get-tuple-element.235.hidden, bf16[256,1024]{1,0:T(8,128)(2,1)} %get-tuple-element.236.mix), custom_call_target="tpu_custom_call" | custom-call | flops 1 | bytes 1 | tf_op jit(solution)/shard_map/pallas_call | solution.py:350
  205.2 3.9 %collective-permute-start.19 = (bf16[2,25,1024]{2,1,0:T(8,128)(2,1)S(1)}, bf16[2,25,1024]{2,1,0:T(8,128)(2,1)S(1)}, u32[]{:S(2)}, u32[]{:S(2)}) collective-permute-start(bf16[2,25,1024]{2,1,0:T(8,128)(2,1)S(1)} %convert_element_type.81), channel_id=1, source_target_pairs={{0,4},{4,0},{8,12},{12,8},{16,20},{20,16},{24,28},{28,24},{1,5},{5... | collective-permute-start | bytes 307208 | tf_op jit(solution)/shard_map/ppermute | solution.py:380
  210.2 1.7 collective-permute-start.18
  212.5 7.8 %shard_map.88 = f32[2,25,1024]{2,1,0:T(8,128)} custom-call(s32[5]{0:T(128)} %stack.40.scalars, bf16[256,1024]{1,0:T(8,128)(2,1)} %get-tuple-element.244.x.refs_1_, bf16[256,1024]{1,0:T(8,128)(2,1)} %get-tuple-element.231.lin, bf16[256,1024]{1,0:T(8,128)(2,1)} %get-tuple-element.232.hidden, bf16[256,1024]{1,0:T(8,128)(2,1)} %get-tuple-element.233.mix), custom_call_target="tpu_custom_call" | custom-call | flops 1 | bytes 1 | tf_op jit(solution)/shard_map/pallas_call | solution.py:350
  221.3 1.3 collective-permute-done.20
  223.9 1.9 shard_map.87
  225.8 2.5 %collective-permute-done.21 = bf16[2,25,1024]{2,1,0:T(8,128)(2,1)S(1)} collective-permute-done((bf16[2,25,1024]{2,1,0:T(8,128)(2,1)S(1)}, bf16[2,25,1024]{2,1,0:T(8,128)(2,1)S(1)}, u32[]{:S(2)}, u32[]{:S(2)}) %collective-permute-start.21) | collective-permute-done | bytes 102432 | tf_op jit(solution)/shard_map/ppermute | solution.py:380
  (89 shorter events, 20.9 us)
Async XLA Ops:
  0.6 39.9 %copy-start = (bf16[2,1,16,16,1024]{4,3,2,1,0:T(8,128)(2,1)S(1)}, bf16[2,1,16,16,1024]{4,3,2,1,0:T(8,128)(2,1)}, u32[]{:S(2)}) copy-start(bf16[2,1,16,16,1024]{4,3,2,1,0:T(8,128)(2,1)} %param.6) | copy-start | bytes 3145732
  0.6 31.1 %copy-start.13 = (f32[1,2,25,1024]{3,1,2,0:T(2,128)S(1)}, f32[1,2,25,1024]{3,1,2,0:T(2,128)}, u32[]{:S(2)}) copy-start(f32[1,2,25,1024]{3,1,2,0:T(2,128)} %param.7) | copy-start | bytes 614404
  2.3 38.3 %copy-start.1 = (bf16[1,256,2,1024]{3,1,2,0:T(8,128)(2,1)}, bf16[1,256,2,1024]{3,1,2,0:T(8,128)(2,1)S(1)}, u32[]{:S(2)}) copy-start(bf16[1,256,2,1024]{3,1,2,0:T(8,128)(2,1)S(1)} %copy.52) | copy-start | bytes 3145732
  2.3 26.2 %collective-permute-start.4 = (bf16[2,256,1024]{2,1,0:T(8,128)(2,1)S(1)}, bf16[2,256,1024]{2,1,0:T(8,128)(2,1)S(1)}, u32[]{:S(2)}, u32[]{:S(2)}) collective-permute-start(bf16[2,256,1024]{2,1,0:T(8,128)(2,1)S(1)} %bitcast.55), channel_id=1, source_target_pairs={{0,2},{1,3},{2,0},{3,1},{4,6},{5,7},{6,4},{7,5},{8,10},{9,11},{10,... | collective-permute-start | bytes 3145736 | tf_op jit(solution)/shard_map/ppermute | solution.py:380
  5.3 26.6 %collective-permute-start = (bf16[2,256,1024]{2,1,0:T(8,128)(2,1)S(1)}, bf16[2,256,1024]{2,1,0:T(8,128)(2,1)}, u32[]{:S(2)}, u32[]{:S(2)}) collective-permute-start(bf16[2,256,1024]{2,1,0:T(8,128)(2,1)S(1)} %bitcast.56), channel_id=1, source_target_pairs={{0,4},{4,0},{8,12},{12,8},{16,20},{20,16},{24,28},{28,24},{1,5},{5... | collective-permute-start | bytes 3145736 | tf_op jit(solution)/shard_map/ppermute | solution.py:380
  6.8 34.6 %collective-permute-start.3 = (bf16[2,256,1024]{2,1,0:T(8,128)(2,1)S(1)}, bf16[2,256,1024]{2,1,0:T(8,128)(2,1)}, u32[]{:S(2)}, u32[]{:S(2)}) collective-permute-start(bf16[2,256,1024]{2,1,0:T(8,128)(2,1)S(1)} %bitcast.57), channel_id=1, source_target_pairs={{0,1},{1,0},{2,3},{3,2},{4,5},{5,4},{6,7},{7,6},{8,9},{9,8},{10,11... | collective-permute-start | bytes 3145736 | tf_op jit(solution)/shard_map/ppermute | solution.py:380
  28.5 12.1 %copy-start.5 = (bf16[2,256,1024]{2,1,0:T(8,128)(2,1)}, bf16[2,256,1024]{2,1,0:T(8,128)(2,1)S(1)}, u32[]{:S(2)}) copy-start(bf16[2,256,1024]{2,1,0:T(8,128)(2,1)S(1)} %collective-permute-done.4.refs_3_.refs_9_) | copy-start | bytes 3145732
  28.5 12.9 %collective-permute-start.5 = (bf16[2,256,1024]{2,1,0:T(8,128)(2,1)S(1)}, bf16[2,256,1024]{2,1,0:T(8,128)(2,1)}, u32[]{:S(2)}, u32[]{:S(2)}) collective-permute-start(bf16[2,256,1024]{2,1,0:T(8,128)(2,1)S(1)} %collective-permute-done.4.refs_3_.refs_9_), channel_id=1, source_target_pairs={{0,1},{1,0},{2,3},{3,2},{4,5},{5,4},{6,7},{7,6},{8,9},{9,8},{10,11... | collective-permute-start | bytes 3145736 | tf_op jit(solution)/shard_map/ppermute | solution.py:380
  31.9 4.5 %copy-start.2 = (f32[2,26,1024]{2,1,0:T(8,128)}, f32[2,26,1024]{2,1,0:T(8,128)S(1)}, u32[]{:S(2)}) copy-start(f32[2,26,1024]{2,1,0:T(8,128)S(1)} %concatenate.27.k.refs_0_.refs_5_) | copy-start | bytes 638980
  31.9 26.9 %collective-permute-start.6 = (bf16[2,256,1024]{2,1,0:T(8,128)(2,1)}, bf16[2,256,1024]{2,1,0:T(8,128)(2,1)}, u32[]{:S(2)}, u32[]{:S(2)}) collective-permute-start(bf16[2,256,1024]{2,1,0:T(8,128)(2,1)} %collective-permute-done.refs_0_.refs_11_), channel_id=1, source_target_pairs={{0,2},{1,3},{2,0},{3,1},{4,6},{5,7},{6,4},{7,5},{8,10},{9,11},{10,... | collective-permute-start | bytes 3145736 | tf_op jit(solution)/shard_map/ppermute | solution.py:380
  33.7 19.6 %collective-permute-start.1 = (bf16[256,1024]{1,0:T(8,128)(2,1)}, bf16[256,1024]{1,0:T(8,128)(2,1)}, u32[]{:S(2)}, u32[]{:S(2)}) collective-permute-start(bf16[256,1024]{1,0:T(8,128)(2,1)} %get-tuple-element.153.x), channel_id=1, source_target_pairs={{0,4},{4,0},{8,12},{12,8},{16,20},{20,16},{24,28},{28,24},{1,5},{5... | collective-permute-start | bytes 1572872 | tf_op jit(solution)/shard_map/ppermute | solution.py:380
  35.2 18.1 %collective-permute-start.2 = (f32[2,26,1024]{2,1,0:T(8,128)S(1)}, f32[2,26,1024]{2,1,0:T(8,128)}, u32[]{:S(2)}, u32[]{:S(2)}) collective-permute-start(f32[2,26,1024]{2,1,0:T(8,128)S(1)} %concatenate.27.k.refs_0_.refs_5_), channel_id=1, source_target_pairs={{0,4},{4,0},{8,12},{12,8},{16,20},{20,16},{24,28},{28,24},{1,5},{5... | collective-permute-start | bytes 638984 | tf_op jit(solution)/shard_map/ppermute | solution.py:380
  58.8 2.9 %collective-permute-start.7 = (bf16[2,256,1024]{2,1,0:T(8,128)(2,1)}, bf16[2,256,1024]{2,1,0:T(8,128)(2,1)S(1)}, u32[]{:S(2)}, u32[]{:S(2)}) collective-permute-start(bf16[2,256,1024]{2,1,0:T(8,128)(2,1)} %collective-permute-done.refs_0_.refs_11_), channel_id=1, source_target_pairs={{0,1},{1,0},{2,3},{3,2},{4,5},{5,4},{6,7},{7,6},{8,9},{9,8},{10,11... | collective-permute-start | bytes 3145736 | tf_op jit(solution)/shard_map/ppermute | solution.py:380
  58.8 4.4 %collective-permute-start.8 = (bf16[2,256,1024]{2,1,0:T(8,128)(2,1)}, bf16[2,256,1024]{2,1,0:T(8,128)(2,1)S(1)}, u32[]{:S(2)}, u32[]{:S(2)}) collective-permute-start(bf16[2,256,1024]{2,1,0:T(8,128)(2,1)} %collective-permute-done.6.refs_2_.refs_13_), channel_id=1, source_target_pairs={{0,1},{1,0},{2,3},{3,2},{4,5},{5,4},{6,7},{7,6},{8,9},{9,8},{10,11... | collective-permute-start | bytes 3145736 | tf_op jit(solution)/shard_map/ppermute | solution.py:380
  69.2 2.8 %copy-start.4 = (bf16[256,1024]{1,0:T(8,128)(2,1)S(1)}, bf16[256,1024]{1,0:T(8,128)(2,1)}, u32[]{:S(2)}) copy-start(bf16[256,1024]{1,0:T(8,128)(2,1)} %shard_map.76.start) | copy-start | bytes 1572868
  70.4 13.4 %collective-permute-start.9 = (bf16[256,1024]{1,0:T(8,128)(2,1)}, bf16[256,1024]{1,0:T(8,128)(2,1)}, u32[]{:S(2)}, u32[]{:S(2)}) collective-permute-start(bf16[256,1024]{1,0:T(8,128)(2,1)} %get-tuple-element.132), channel_id=1, source_target_pairs={{24,16},{28,20},{25,17},{29,21},{26,18},{30,22},{27,19},{31,23}} | collective-permute-start | bytes 1572872 | tf_op jit(solution)/shard_map/ppermute | solution.py:471
  83.8 1.9 copy-start.3
  83.8 1.9 copy-start.11
  85.0 1.0 collective-permute-start.10
  87.8 73.0 %collective-permute-start.11 = (bf16[256,1024]{1,0:T(8,128)(2,1)}, bf16[256,1024]{1,0:T(8,128)(2,1)}, u32[]{:S(2)}, u32[]{:S(2)}) collective-permute-start(bf16[256,1024]{1,0:T(8,128)(2,1)} %get-tuple-element.189), channel_id=1, source_target_pairs={{8,0},{12,4},{9,1},{13,5},{10,2},{14,6},{11,3},{15,7}} | collective-permute-start | bytes 1572872 | tf_op jit(solution)/shard_map/ppermute | solution.py:471
  168.9 13.6 %collective-permute-start.12 = (bf16[256,1024]{1,0:T(8,128)(2,1)}, bf16[256,1024]{1,0:T(8,128)(2,1)S(1)}, u32[]{:S(2)}, u32[]{:S(2)}) collective-permute-start(bf16[256,1024]{1,0:T(8,128)(2,1)} %get-tuple-element.213), channel_id=1, source_target_pairs={{0,4},{4,0},{8,12},{12,8},{16,20},{20,16},{24,28},{28,24},{1,5},{5... | collective-permute-start | bytes 1572872 | tf_op jit(solution)/shard_map/ppermute | solution.py:380
  182.0 12.2 %collective-permute-start.15 = (bf16[256,1024]{1,0:T(8,128)(2,1)}, bf16[256,1024]{1,0:T(8,128)(2,1)S(1)}, u32[]{:S(2)}, u32[]{:S(2)}) collective-permute-start(bf16[256,1024]{1,0:T(8,128)(2,1)} %get-tuple-element.216), channel_id=1, source_target_pairs={{0,4},{4,0},{8,12},{12,8},{16,20},{20,16},{24,28},{28,24},{1,5},{5... | collective-permute-start | bytes 1572872 | tf_op jit(solution)/shard_map/ppermute | solution.py:380
  183.5 12.3 %copy-start.6 = (bf16[256,1024]{1,0:T(8,128)(2,1)S(1)}, bf16[256,1024]{1,0:T(8,128)(2,1)}, u32[]{:S(2)}) copy-start(bf16[256,1024]{1,0:T(8,128)(2,1)} %get-tuple-element.222) | copy-start | bytes 1572868
  183.5 14.2 %collective-permute-start.13 = (bf16[512,1024]{1,0:T(8,128)(2,1)S(1)}, bf16[512,1024]{1,0:T(8,128)(2,1)S(1)}, u32[]{:S(2)}, u32[]{:S(2)}) collective-permute-start(bf16[512,1024]{1,0:T(8,128)(2,1)S(1)} %add_convert_fusion.1), channel_id=1, source_target_pairs={{0,1},{1,0},{2,3},{3,2},{4,5},{5,4},{6,7},{7,6},{8,9},{9,8},{10,11... | collective-permute-start | bytes 3145736 | tf_op jit(solution)/shard_map/ppermute | solution.py:380
  194.2 14.9 %collective-permute-start.16 = (bf16[256,1024]{1,0:T(8,128)(2,1)}, bf16[256,1024]{1,0:T(8,128)(2,1)S(1)}, u32[]{:S(2)}, u32[]{:S(2)}) collective-permute-start(bf16[256,1024]{1,0:T(8,128)(2,1)} %get-tuple-element.218), channel_id=1, source_target_pairs={{0,4},{4,0},{8,12},{12,8},{16,20},{20,16},{24,28},{28,24},{1,5},{5... | collective-permute-start | bytes 1572872 | tf_op jit(solution)/shard_map/ppermute | solution.py:380
  196.3 2.7 %collective-permute-start.17 = (bf16[512,1024]{1,0:T(8,128)(2,1)S(1)}, bf16[512,1024]{1,0:T(8,128)(2,1)S(1)}, u32[]{:S(2)}, u32[]{:S(2)}) collective-permute-start(bf16[512,1024]{1,0:T(8,128)(2,1)S(1)} %add_convert_fusion), channel_id=1, source_target_pairs={{0,1},{1,0},{2,3},{3,2},{4,5},{5,4},{6,7},{7,6},{8,9},{9,8},{10,11... | collective-permute-start | bytes 3145736 | tf_op jit(solution)/shard_map/ppermute | solution.py:380
  198.1 14.4 %collective-permute-start.14 = (bf16[256,1024]{1,0:T(8,128)(2,1)S(1)}, bf16[256,1024]{1,0:T(8,128)(2,1)S(1)}, u32[]{:S(2)}, u32[]{:S(2)}) collective-permute-start(bf16[256,1024]{1,0:T(8,128)(2,1)S(1)} %get-tuple-element.242), channel_id=1, source_target_pairs={{0,2},{1,3},{2,0},{3,1},{4,6},{5,7},{6,4},{7,5},{8,10},{9,11},{10,... | collective-permute-start | bytes 1572872 | tf_op jit(solution)/shard_map/ppermute | solution.py:380
  199.3 9.8 %copy-start.10 = (bf16[256,1024]{1,0:T(8,128)(2,1)S(1)}, bf16[256,1024]{1,0:T(8,128)(2,1)}, u32[]{:S(2)}) copy-start(bf16[256,1024]{1,0:T(8,128)(2,1)} %get-tuple-element.219) | copy-start | bytes 1572868
  205.2 15.0 %collective-permute-start.19 = (bf16[2,25,1024]{2,1,0:T(8,128)(2,1)S(1)}, bf16[2,25,1024]{2,1,0:T(8,128)(2,1)S(1)}, u32[]{:S(2)}, u32[]{:S(2)}) collective-permute-start(bf16[2,25,1024]{2,1,0:T(8,128)(2,1)S(1)} %convert_element_type.81), channel_id=1, source_target_pairs={{0,4},{4,0},{8,12},{12,8},{16,20},{20,16},{24,28},{28,24},{1,5},{5... | collective-permute-start | bytes 307208 | tf_op jit(solution)/shard_map/ppermute | solution.py:380
  210.2 13.7 %collective-permute-start.18 = (bf16[256,1024]{1,0:T(8,128)(2,1)S(1)}, bf16[256,1024]{1,0:T(8,128)(2,1)S(1)}, u32[]{:S(2)}, u32[]{:S(2)}) collective-permute-start(bf16[256,1024]{1,0:T(8,128)(2,1)S(1)} %get-tuple-element.228), channel_id=1, source_target_pairs={{0,2},{1,3},{2,0},{3,1},{4,6},{5,7},{6,4},{7,5},{8,10},{9,11},{10,... | collective-permute-start | bytes 1572872 | tf_op jit(solution)/shard_map/ppermute | solution.py:380
  221.2 1.4 collective-permute-start.20
  222.7 5.6 %collective-permute-start.21 = (bf16[2,25,1024]{2,1,0:T(8,128)(2,1)S(1)}, bf16[2,25,1024]{2,1,0:T(8,128)(2,1)S(1)}, u32[]{:S(2)}, u32[]{:S(2)}) collective-permute-start(bf16[2,25,1024]{2,1,0:T(8,128)(2,1)S(1)} %add_convert_fusion.4), channel_id=1, source_target_pairs={{0,2},{1,3},{2,0},{3,1},{4,6},{5,7},{6,4},{7,5},{8,10},{9,11},{10,... | collective-permute-start | bytes 307208 | tf_op jit(solution)/shard_map/ppermute | solution.py:380
  (5 other events, 6.1 us)
where the time goes:
time: 228 us; the launch traced here: 229 us
  waiting for transfers between devices  118 us (52%)
  Pallas kernels  67.3 us (30%)
  starting transfers between devices  22.9 us (10%)
  local copies, waits for them, and re-layouts  10.8 us (5%)
  other arithmetic  3.96 us (2%)
  matrix products  3.65 us (2%)
  between operations  2.49 us (1%)
    ppermute x3, waiting for transfers between devices, body(): lax.ppermute(leaving, 'segment', [(2 * source + h, 2 * source - 2 + h) fo...  71.7 us
    ppermute x19, waiting for transfers between devices, swap(): lax.ppermute(value, axis, [(source, source ^ bit) for source in range(cou...  46.4 us
    pallas_call x5, Pallas kernels, chain(): pl.pallas_call(functools.partial(chain_kernel, pair=pair, visits=visits,...  21.7 us
    pallas_call x3, Pallas kernels, forward_rest(): pl.pallas_call(functools.partial(rest_kernel, slot=slot, side=side, parts...  19.9 us
    ppermute x19, starting transfers between devices, swap(): lax.ppermute(value, axis, [(source, source ^ bit) for source in range(cou...  19.4 us
    pallas_call x2, Pallas kernels, tap_sums(): pl.pallas_call(functools.partial(taps_kernel, slot=slot, side=side), in_s...  12.7 us
    pallas_call x3, Pallas kernels, forward_start(): pl.pallas_call(functools.partial(start_kernel, slot=slot, side=side), in_...  11.1 us
  transfers between devices with their start and end apart: 22, of which 12 were waited for; matrix products, arithmetic and copies ran while one was open for 6% of the time, Pallas kernels for 22%

commit v1 on v0

--- a/solution.py
+++ b/solution.py
@@ -426,13 +426,14 @@
     x_all = checkpoint[0].reshape(micro, rows, channels)
     x_own = lax.dynamic_index_in_dim(x_all, half, 0, keepdims=False)
     x_other = lax.dynamic_index_in_dim(x_all, 1 - half, 0, keepdims=False)
-    kind_row = jnp.full((2, 1, channels), genotype[0].astype(jnp.float32))
-    k_own = jnp.concatenate([depthwise[0], kind_row], axis=1)
+    k_own = depthwise[0]
 
     far_bits = [1 << bit for bit in range(dp.bit_length() - 2, 0, -1)]
     own_rows = jnp.swapaxes(pointwise[0], 0, 1)
     own_held = doubled([(0, own_rows)], far_bits)
-    partner_rows, x_sent, k_sent = lax.optimization_barrier((swap(own_rows, "segment", 1), x_other, k_own))
+    partner_rows, x_sent, k_sent, kind_partner = lax.optimization_barrier(
+        (swap(own_rows, "segment", 1), x_other, k_own, swap(genotype, "segment", 1))
+    )
     x_partner = swap(x_sent, "segment", 1)
     k_partner = swap(k_sent, "segment", 1)
     partner_held = doubled([(0, partner_rows)], far_bits)
@@ -441,11 +442,10 @@
     first_own = forward_start(scalars_own, x_own, k_own, 0, side)
     hidden_own, slope_own, mixed_own = forward_rest(scalars_own, first_own, k_own, own_blocks, 0, side, True)
     upstream = lax.dynamic_index_in_dim(cotangent, half, 0, keepdims=False).reshape(rows, channels)
-    x_partner, k_partner, slope_own, upstream = lax.optimization_barrier(
-        (x_partner, k_partner, slope_own, upstream)
+    scalars = jnp.stack([turned, genotype[0], kind_partner[0], half, pair]).astype(jnp.int32)
+    x_partner, k_partner, slope_own, upstream, scalars = lax.optimization_barrier(
+        (x_partner, k_partner, slope_own, upstream, scalars)
     )
-    kind_partner = k_partner[0, TAPS, 0].astype(jnp.int32)
-    scalars = jnp.stack([turned, genotype[0], kind_partner, half, pair]).astype(jnp.int32)
     first_partner = forward_start(scalars, x_partner, k_partner, 1, side)
     far, first_partner = lax.optimization_barrier(([part for _, part in partner_held], first_partner))
     partner_held = [(mask, part) for (mask, _), part in zip(partner_held, far)]

time: 228 us -> 225 us (0.987); the launches traced: 229 us -> 223 us
  Pallas kernels: 67.3 us -> 63.4 us
  starting transfers between devices: 22.9 us -> 20.6 us
    ppermute x19 -> x20, waiting for transfers between devices: 46.4 us -> 49.7 us  [swap(): lax.ppermute(value, axis, [(source, source ^ bit) for source in range(cou...]
    pallas_call x3, Pallas kernels: 19.9 us -> 17.3 us  [forward_rest(): pl.pallas_call(functools.partial(rest_kernel, slot=slot, side=side, parts...]
    ppermute x19 -> x20, starting transfers between devices: 19.4 us -> 17 us  [swap(): lax.ppermute(value, axis, [(source, source ^ bit) for source in range(cou...]
  transfers between devices with their start and end apart: 22 -> 23, of which waited for: 12 -> 11; matrix products, arithmetic and copies ran while one was open for 6% -> 6% of each run, Pallas kernels for 22% -> 20%
where the time goes in v1:
time: 225 us; the launch traced here: 223 us
  waiting for transfers between devices  119 us (53%)
  Pallas kernels  63.4 us (28%)
  starting transfers between devices  20.6 us (9%)
  local copies, waits for them, and re-layouts  10 us (4%)
  other arithmetic  3.97 us (2%)
  matrix products  3.66 us (2%)
    ppermute x3, waiting for transfers between devices, body(): lax.ppermute(leaving, 'segment', [(2 * source + h, 2 * source - 2 + h) fo...  69.4 us
    ppermute x20, waiting for transfers between devices, swap(): lax.ppermute(value, axis, [(source, source ^ bit) for source in range(cou...  49.7 us
    pallas_call x5, Pallas kernels, chain(): pl.pallas_call(functools.partial(chain_kernel, pair=pair, visits=visits,...  21.7 us
    pallas_call x3, Pallas kernels, forward_rest(): pl.pallas_call(functools.partial(rest_kernel, slot=slot, side=side, parts...  17.3 us
    ppermute x20, starting transfers between devices, swap(): lax.ppermute(value, axis, [(source, source ^ bit) for source in range(cou...  17 us
    pallas_call x2, Pallas kernels, tap_sums(): pl.pallas_call(functools.partial(taps_kernel, slot=slot, side=side), in_s...  12.7 us
    pallas_call x3, Pallas kernels, forward_start(): pl.pallas_call(functools.partial(start_kernel, slot=slot, side=side), in_...  9.85 us
  transfers between devices with their start and end apart: 23, of which 11 were waited for; matrix products, arithmetic and copies ran while one was open for 6% of the time, Pallas kernels for 20%

profile of v1, /device:TPU:0, one launch (start us, length us, event | category | flops | bytes accessed | tf_op | source)
XLA Modules:
  0.0 222.6 jit_solution(14355610685393928169)
XLA Ops:
  0.6 1.6 copy.52
  2.2 3.0 %collective-permute-start.5 = (bf16[2,256,1024]{2,1,0:T(8,128)(2,1)S(1)}, bf16[2,256,1024]{2,1,0:T(8,128)(2,1)S(1)}, u32[]{:S(2)}, u32[]{:S(2)}) collective-permute-start(bf16[2,256,1024]{2,1,0:T(8,128)(2,1)S(1)} %bitcast.53), channel_id=1, source_target_pairs={{0,2},{1,3},{2,0},{3,1},{4,6},{5,7},{6,4},{7,5},{8,10},{9,11},{10,... | collective-permute-start | bytes 3145736 | tf_op jit(solution)/shard_map/ppermute | solution.py:380
  5.3 1.5 collective-permute-start
  7.3 21.1 %collective-permute-done.5.refs_3_.refs_9_ = bf16[2,256,1024]{2,1,0:T(8,128)(2,1)S(1)} collective-permute-done((bf16[2,256,1024]{2,1,0:T(8,128)(2,1)S(1)}, bf16[2,256,1024]{2,1,0:T(8,128)(2,1)S(1)}, u32[]{:S(2)}, u32[]{:S(2)}) %collective-permute-start.5) | collective-permute-done | bytes 1048608 | tf_op jit(solution)/shard_map/ppermute | solution.py:380
  28.4 2.6 %dynamic-slice_bitcast_fusion = (bf16[256,1024]{1,0:T(8,128)(2,1)}, bf16[256,1024]{1,0:T(8,128)(2,1)}) fusion(bf16[2,256,1024]{2,1,0:T(8,128)(2,1)} %bitcast.79, s32[]{:T(128)S(6)} %select_n.88, s32[]{:T(128)S(6)} %select_n.86), kind=kLoop, calls=%fused_computation.12 | loop fusion | bytes 2097160 | tf_op jit(solution)/shard_map/jit(dynamic_index_in_dim)/squeeze | solution.py:427
  31.2 1.8 collective-permute-start.7
  33.0 1.5 collective-permute-start.2
  36.4 2.9 %shard_map.76.start = bf16[256,1024]{1,0:T(8,128)(2,1)} custom-call(s32[5]{0:T(128)} %stack.35.scalars, bf16[256,1024]{1,0:T(8,128)(2,1)} %get-tuple-element.248.x.refs_1_, f32[2,25,1024]{2,1,0:T(8,128)} %bitcast.66), custom_call_target="tpu_custom_call" | custom-call | flops 1 | bytes 1 | tf_op jit(solution)/shard_map/pallas_call | solution.py:281
  41.3 6.2 %shard_map.77 = (bf16[256,1024]{1,0:T(8,128)(2,1)}, bf16[256,1024]{1,0:T(8,128)(2,1)}, bf16[256,1024]{1,0:T(8,128)(2,1)}) custom-call(s32[5]{0:T(128)} %stack.35.scalars, bf16[256,1024]{1,0:T(8,128)(2,1)} %shard_map.76.start, f32[2,25,1024]{2,1,0:T(8,128)} %bitcast.67, bf16[2,256,1024]{2,1,0:T(8,128)(2,1)} %bitcast.56, ...), custom_call_target="tpu_custom_call" | custom-call | flops 1 | bytes 1 | tf_op jit(solution)/shard_map/pallas_call | solution.py:296
  47.5 5.1 %collective-permute-done.3.k.refs_6_ = f32[2,25,1024]{2,1,0:T(8,128)} collective-permute-done((f32[2,25,1024]{2,1,0:T(8,128)S(1)}, f32[2,25,1024]{2,1,0:T(8,128)}, u32[]{:S(2)}, u32[]{:S(2)}) %collective-permute-start.3) | collective-permute-done | bytes 204832 | tf_op jit(solution)/shard_map/ppermute | solution.py:380
  52.6 4.1 %shard_map.78.start = bf16[256,1024]{1,0:T(8,128)(2,1)} custom-call(s32[5]{0:T(128)} %stack.36.scalars, bf16[256,1024]{1,0:T(8,128)(2,1)} %collective-permute-done.2.x.refs_2_, f32[2,25,1024]{2,1,0:T(8,128)} %collective-permute-done.3.k.refs_6_), custom_call_target="tpu_custom_call" | custom-call | flops 1 | bytes 1 | tf_op jit(solution)/shard_map/pallas_call | solution.py:281
  57.3 2.4 %collective-permute-done.8.refs_1_.refs_12_ = bf16[2,256,1024]{2,1,0:T(8,128)(2,1)S(1)} collective-permute-done((bf16[2,256,1024]{2,1,0:T(8,128)(2,1)}, bf16[2,256,1024]{2,1,0:T(8,128)(2,1)S(1)}, u32[]{:S(2)}, u32[]{:S(2)}) %collective-permute-start.8) | collective-permute-done | bytes 1048608 | tf_op jit(solution)/shard_map/ppermute | solution.py:380
  59.6 1.5 collective-permute-done.9.refs_3_.refs_14_
  62.1 5.0 %shard_map.79 = (bf16[256,1024]{1,0:T(8,128)(2,1)}, bf16[256,1024]{1,0:T(8,128)(2,1)}) custom-call(s32[5]{0:T(128)} %stack.36.scalars, bf16[256,1024]{1,0:T(8,128)(2,1)} %shard_map.78.start, bf16[2,256,1024]{2,1,0:T(8,128)(2,1)} %collective-permute-done.refs_0_.refs_11_, bf16[2,256,1024]{2,1,0:T(8,128)(2,1)} %copy-done.8, ...), custom_call_target="tpu_custom_call" | custom-call | flops 1 | bytes 1 | tf_op jit(solution)/shard_map/pallas_call | solution.py:296
  68.3 1.6 collective-permute-start.10
  70.1 2.9 %shard_map.81.start = bf16[256,1024]{1,0:T(8,128)(2,1)} custom-call(s32[5]{0:T(128)} %stack.35.scalars, bf16[256,1024]{1,0:T(8,128)(2,1)} %get-tuple-element.157.x, f32[2,25,1024]{2,1,0:T(8,128)} %bitcast.69), custom_call_target="tpu_custom_call" | custom-call | flops 1 | bytes 1 | tf_op jit(solution)/shard_map/pallas_call | solution.py:281
  73.0 6.1 %shard_map.82 = (bf16[256,1024]{1,0:T(8,128)(2,1)}, bf16[256,1024]{1,0:T(8,128)(2,1)}, bf16[256,1024]{1,0:T(8,128)(2,1)}) custom-call(s32[5]{0:T(128)} %stack.35.scalars, bf16[256,1024]{1,0:T(8,128)(2,1)} %shard_map.81.start, f32[2,25,1024]{2,1,0:T(8,128)} %bitcast.70, bf16[2,256,1024]{2,1,0:T(8,128)(2,1)} %bitcast.58, ...), custom_call_target="tpu_custom_call" | custom-call | flops 1 | bytes 1 | tf_op jit(solution)/shard_map/pallas_call | solution.py:296
  84.5 69.4 %collective-permute-done.12.refs_0_ = bf16[256,1024]{1,0:T(8,128)(2,1)} collective-permute-done((bf16[256,1024]{1,0:T(8,128)(2,1)}, bf16[256,1024]{1,0:T(8,128)(2,1)}, u32[]{:S(2)}, u32[]{:S(2)}) %collective-permute-start.12) | collective-permute-done | bytes 524320 | tf_op jit(solution)/shard_map/ppermute | solution.py:471
  153.9 10.6 %shard_map.85 = (bf16[256,1024]{1,0:T(8,128)(2,1)}, bf16[256,1024]{1,0:T(8,128)(2,1)}, bf16[256,1024]{1,0:T(8,128)(2,1)}, bf16[256,1024]{1,0:T(8,128)(2,1)}, bf1...) custom-call(s32[5]{0:T(128)} %stack.36.scalars, ...), custom_call_target="tpu_custom_call", output_to_operand_aliasing={{0}: (16, {}), {1}: (17, {}), {2}: (18, {}), {3}: (19, {}),... | custom-call | flops 10000000000 | bytes 12582912 | tf_op jit(solution)/shard_map/pallas_call | solution.py:203
  164.5 1.4 collective-permute-start.13
  166.0 7.8 %shard_map.86 = (bf16[256,1024]{1,0:T(8,128)(2,1)}, bf16[256,1024]{1,0:T(8,128)(2,1)}, bf16[256,1024]{1,0:T(8,128)(2,1)}, bf16[256,1024]{1,0:T(8,128)(2,1)}, bf1...) custom-call(s32[5]{0:T(128)} %stack.36.scalars, ...), custom_call_target="tpu_custom_call", output_to_operand_aliasing={{0}: (16, {}), {1}: (17, {}), {2}: (18, {}), {3}: (19, {}),... | custom-call | flops 10000000000 | bytes 12582912 | tf_op jit(solution)/shard_map/pallas_call | solution.py:203
  174.5 4.8 %collective-permute-done.13 = bf16[256,1024]{1,0:T(8,128)(2,1)S(1)} collective-permute-done((bf16[256,1024]{1,0:T(8,128)(2,1)}, bf16[256,1024]{1,0:T(8,128)(2,1)S(1)}, u32[]{:S(2)}, u32[]{:S(2)}) %collective-permute-start.13) | collective-permute-done | bytes 524320 | tf_op jit(solution)/shard_map/ppermute | solution.py:380
  180.3 8.0 %collective-permute-done.16 = bf16[256,1024]{1,0:T(8,128)(2,1)S(1)} collective-permute-done((bf16[256,1024]{1,0:T(8,128)(2,1)}, bf16[256,1024]{1,0:T(8,128)(2,1)S(1)}, u32[]{:S(2)}, u32[]{:S(2)}) %collective-permute-start.16) | collective-permute-done | bytes 524320 | tf_op jit(solution)/shard_map/ppermute | solution.py:380
  188.3 1.3 collective-permute-start.17
  192.4 1.7 collective-permute-start.15
  194.8 7.8 %shard_map.89 = f32[2,25,1024]{2,1,0:T(8,128)} custom-call(s32[5]{0:T(128)} %stack.36.scalars, bf16[256,1024]{1,0:T(8,128)(2,1)} %collective-permute-done.2.x.refs_2_, bf16[256,1024]{1,0:T(8,128)(2,1)} %get-tuple-element.238.lin, bf16[256,1024]{1,0:T(8,128)(2,1)} %get-tuple-element.239.hidden, bf16[256,1024]{1,0:T(8,128)(2,1)} %get-tuple-element.240.mix), custom_call_target="tpu_custom_call" | custom-call | flops 1 | bytes 1 | tf_op jit(solution)/shard_map/pallas_call | solution.py:350
  205.3 1.5 collective-permute-done.15.second_came
  206.7 4.9 %shard_map.88 = f32[2,25,1024]{2,1,0:T(8,128)} custom-call(s32[5]{0:T(128)} %stack.36.scalars, bf16[256,1024]{1,0:T(8,128)(2,1)} %get-tuple-element.248.x.refs_1_, bf16[256,1024]{1,0:T(8,128)(2,1)} %get-tuple-element.235.lin, bf16[256,1024]{1,0:T(8,128)(2,1)} %get-tuple-element.236.hidden, bf16[256,1024]{1,0:T(8,128)(2,1)} %get-tuple-element.237.mix), custom_call_target="tpu_custom_call" | custom-call | flops 1 | bytes 1 | tf_op jit(solution)/shard_map/pallas_call | solution.py:350
  212.7 1.3 collective-permute-done.21
  214.0 1.8 collective-permute-start.22
  215.9 3.8 %collective-permute-done.19.first_came = bf16[256,1024]{1,0:T(8,128)(2,1)S(1)} collective-permute-done((bf16[256,1024]{1,0:T(8,128)(2,1)S(1)}, bf16[256,1024]{1,0:T(8,128)(2,1)S(1)}, u32[]{:S(2)}, u32[]{:S(2)}) %collective-permute-start.19) | collective-permute-done | bytes 524320 | tf_op jit(solution)/shard_map/ppermute | solution.py:380
  219.6 1.9 shard_map.87
  (89 shorter events, 21.9 us)
Async XLA Ops:
  0.6 38.6 %copy-start = (bf16[2,1,16,16,1024]{4,3,2,1,0:T(8,128)(2,1)S(1)}, bf16[2,1,16,16,1024]{4,3,2,1,0:T(8,128)(2,1)}, u32[]{:S(2)}) copy-start(bf16[2,1,16,16,1024]{4,3,2,1,0:T(8,128)(2,1)} %param.6) | copy-start | bytes 3145732
  2.2 37.9 %copy-start.1 = (bf16[1,256,2,1024]{3,1,2,0:T(8,128)(2,1)}, bf16[1,256,2,1024]{3,1,2,0:T(8,128)(2,1)S(1)}, u32[]{:S(2)}) copy-start(bf16[1,256,2,1024]{3,1,2,0:T(8,128)(2,1)S(1)} %copy.52) | copy-start | bytes 3145732
  2.2 26.2 %collective-permute-start.5 = (bf16[2,256,1024]{2,1,0:T(8,128)(2,1)S(1)}, bf16[2,256,1024]{2,1,0:T(8,128)(2,1)S(1)}, u32[]{:S(2)}, u32[]{:S(2)}) collective-permute-start(bf16[2,256,1024]{2,1,0:T(8,128)(2,1)S(1)} %bitcast.53), channel_id=1, source_target_pairs={{0,2},{1,3},{2,0},{3,1},{4,6},{5,7},{6,4},{7,5},{8,10},{9,11},{10,... | collective-permute-start | bytes 3145736 | tf_op jit(solution)/shard_map/ppermute | solution.py:380
  5.3 25.9 %collective-permute-start = (bf16[2,256,1024]{2,1,0:T(8,128)(2,1)S(1)}, bf16[2,256,1024]{2,1,0:T(8,128)(2,1)}, u32[]{:S(2)}, u32[]{:S(2)}) collective-permute-start(bf16[2,256,1024]{2,1,0:T(8,128)(2,1)S(1)} %bitcast.54), channel_id=1, source_target_pairs={{0,4},{4,0},{8,12},{12,8},{16,20},{20,16},{24,28},{28,24},{1,5},{5... | collective-permute-start | bytes 3145736 | tf_op jit(solution)/shard_map/ppermute | solution.py:380
  6.8 34.6 %collective-permute-start.4 = (bf16[2,256,1024]{2,1,0:T(8,128)(2,1)S(1)}, bf16[2,256,1024]{2,1,0:T(8,128)(2,1)}, u32[]{:S(2)}, u32[]{:S(2)}) collective-permute-start(bf16[2,256,1024]{2,1,0:T(8,128)(2,1)S(1)} %bitcast.55), channel_id=1, source_target_pairs={{0,1},{1,0},{2,3},{3,2},{4,5},{5,4},{6,7},{7,6},{8,9},{9,8},{10,11... | collective-permute-start | bytes 3145736 | tf_op jit(solution)/shard_map/ppermute | solution.py:380
  6.8 24.4 %collective-permute-start.1 = (s32[1]{0:T(128)}, s32[1]{0:T(128)}, u32[]{:S(2)}, u32[]{:S(2)}) collective-permute-start(s32[1]{0:T(128)} %param.9), channel_id=1, source_target_pairs={{0,4},{4,0},{8,12},{12,8},{16,20},{20,16},{24,28},{28,24},{1,5},{5... | collective-permute-start | bytes 20 | tf_op jit(solution)/shard_map/ppermute | solution.py:380
  7.3 23.8 %copy-start.13 = (f32[1,2,25,1024]{3,1,2,0:T(2,128)S(1)}, f32[1,2,25,1024]{3,1,2,0:T(2,128)}, u32[]{:S(2)}) copy-start(f32[1,2,25,1024]{3,1,2,0:T(2,128)} %param.7) | copy-start | bytes 614404
  28.4 11.7 %copy-start.5 = (bf16[2,256,1024]{2,1,0:T(8,128)(2,1)}, bf16[2,256,1024]{2,1,0:T(8,128)(2,1)S(1)}, u32[]{:S(2)}) copy-start(bf16[2,256,1024]{2,1,0:T(8,128)(2,1)S(1)} %collective-permute-done.5.refs_3_.refs_9_) | copy-start | bytes 3145732
  28.4 12.9 %collective-permute-start.6 = (bf16[2,256,1024]{2,1,0:T(8,128)(2,1)S(1)}, bf16[2,256,1024]{2,1,0:T(8,128)(2,1)}, u32[]{:S(2)}, u32[]{:S(2)}) collective-permute-start(bf16[2,256,1024]{2,1,0:T(8,128)(2,1)S(1)} %collective-permute-done.5.refs_3_.refs_9_), channel_id=1, source_target_pairs={{0,1},{1,0},{2,3},{3,2},{4,5},{5,4},{6,7},{7,6},{8,9},{9,8},{10,11... | collective-permute-start | bytes 3145736 | tf_op jit(solution)/shard_map/ppermute | solution.py:380
  31.2 5.2 %copy-start.2 = (f32[1,2,25,1024]{3,2,1,0:T(8,128)}, f32[1,2,25,1024]{3,2,1,0:T(8,128)S(1)}, u32[]{:S(2)}) copy-start(f32[1,2,25,1024]{3,2,1,0:T(8,128)S(1)} %copy.53) | copy-start | bytes 614404
  31.2 25.6 %collective-permute-start.7 = (bf16[2,256,1024]{2,1,0:T(8,128)(2,1)}, bf16[2,256,1024]{2,1,0:T(8,128)(2,1)}, u32[]{:S(2)}, u32[]{:S(2)}) collective-permute-start(bf16[2,256,1024]{2,1,0:T(8,128)(2,1)} %collective-permute-done.refs_0_.refs_11_), channel_id=1, source_target_pairs={{0,2},{1,3},{2,0},{3,1},{4,6},{5,7},{6,4},{7,5},{8,10},{9,11},{10,... | collective-permute-start | bytes 3145736 | tf_op jit(solution)/shard_map/ppermute | solution.py:380
  33.0 19.6 %collective-permute-start.2 = (bf16[256,1024]{1,0:T(8,128)(2,1)}, bf16[256,1024]{1,0:T(8,128)(2,1)}, u32[]{:S(2)}, u32[]{:S(2)}) collective-permute-start(bf16[256,1024]{1,0:T(8,128)(2,1)} %get-tuple-element.157.x), channel_id=1, source_target_pairs={{0,4},{4,0},{8,12},{12,8},{16,20},{20,16},{24,28},{28,24},{1,5},{5... | collective-permute-start | bytes 1572872 | tf_op jit(solution)/shard_map/ppermute | solution.py:380
  34.5 18.1 %collective-permute-start.3 = (f32[2,25,1024]{2,1,0:T(8,128)S(1)}, f32[2,25,1024]{2,1,0:T(8,128)}, u32[]{:S(2)}, u32[]{:S(2)}) collective-permute-start(f32[2,25,1024]{2,1,0:T(8,128)S(1)} %bitcast.65), channel_id=1, source_target_pairs={{0,4},{4,0},{8,12},{12,8},{16,20},{20,16},{24,28},{28,24},{1,5},{5... | collective-permute-start | bytes 614408 | tf_op jit(solution)/shard_map/ppermute | solution.py:380
  56.8 2.9 %collective-permute-start.8 = (bf16[2,256,1024]{2,1,0:T(8,128)(2,1)}, bf16[2,256,1024]{2,1,0:T(8,128)(2,1)S(1)}, u32[]{:S(2)}, u32[]{:S(2)}) collective-permute-start(bf16[2,256,1024]{2,1,0:T(8,128)(2,1)} %collective-permute-done.refs_0_.refs_11_), channel_id=1, source_target_pairs={{0,1},{1,0},{2,3},{3,2},{4,5},{5,4},{6,7},{7,6},{8,9},{9,8},{10,11... | collective-permute-start | bytes 3145736 | tf_op jit(solution)/shard_map/ppermute | solution.py:380
  56.8 4.4 %collective-permute-start.9 = (bf16[2,256,1024]{2,1,0:T(8,128)(2,1)}, bf16[2,256,1024]{2,1,0:T(8,128)(2,1)S(1)}, u32[]{:S(2)}, u32[]{:S(2)}) collective-permute-start(bf16[2,256,1024]{2,1,0:T(8,128)(2,1)} %collective-permute-done.7.refs_2_.refs_13_), channel_id=1, source_target_pairs={{0,1},{1,0},{2,3},{3,2},{4,5},{5,4},{6,7},{7,6},{8,9},{9,8},{10,11... | collective-permute-start | bytes 3145736 | tf_op jit(solution)/shard_map/ppermute | solution.py:380
  67.1 2.8 %copy-start.4 = (bf16[256,1024]{1,0:T(8,128)(2,1)S(1)}, bf16[256,1024]{1,0:T(8,128)(2,1)}, u32[]{:S(2)}) copy-start(bf16[256,1024]{1,0:T(8,128)(2,1)} %shard_map.76.start) | copy-start | bytes 1572868
  68.3 10.9 %collective-permute-start.10 = (bf16[256,1024]{1,0:T(8,128)(2,1)}, bf16[256,1024]{1,0:T(8,128)(2,1)}, u32[]{:S(2)}, u32[]{:S(2)}) collective-permute-start(bf16[256,1024]{1,0:T(8,128)(2,1)} %get-tuple-element.136), channel_id=1, source_target_pairs={{24,16},{28,20},{25,17},{29,21},{26,18},{30,22},{27,19},{31,23}} | collective-permute-start | bytes 1572872 | tf_op jit(solution)/shard_map/ppermute | solution.py:471
  80.4 1.0 collective-permute-start.11
  83.1 70.8 %collective-permute-start.12 = (bf16[256,1024]{1,0:T(8,128)(2,1)}, bf16[256,1024]{1,0:T(8,128)(2,1)}, u32[]{:S(2)}, u32[]{:S(2)}) collective-permute-start(bf16[256,1024]{1,0:T(8,128)(2,1)} %get-tuple-element.193), channel_id=1, source_target_pairs={{8,0},{12,4},{9,1},{13,5},{10,2},{14,6},{11,3},{15,7}} | collective-permute-start | bytes 1572872 | tf_op jit(solution)/shard_map/ppermute | solution.py:471
  164.5 14.8 %collective-permute-start.13 = (bf16[256,1024]{1,0:T(8,128)(2,1)}, bf16[256,1024]{1,0:T(8,128)(2,1)S(1)}, u32[]{:S(2)}, u32[]{:S(2)}) collective-permute-start(bf16[256,1024]{1,0:T(8,128)(2,1)} %get-tuple-element.217), channel_id=1, source_target_pairs={{0,4},{4,0},{8,12},{12,8},{16,20},{20,16},{24,28},{28,24},{1,5},{5... | collective-permute-start | bytes 1572872 | tf_op jit(solution)/shard_map/ppermute | solution.py:380
  173.8 6.0 %copy-start.7 = (bf16[256,1024]{1,0:T(8,128)(2,1)S(1)}, bf16[256,1024]{1,0:T(8,128)(2,1)}, u32[]{:S(2)}) copy-start(bf16[256,1024]{1,0:T(8,128)(2,1)} %get-tuple-element.215) | copy-start | bytes 1572868
  173.8 14.5 %collective-permute-start.16 = (bf16[256,1024]{1,0:T(8,128)(2,1)}, bf16[256,1024]{1,0:T(8,128)(2,1)S(1)}, u32[]{:S(2)}, u32[]{:S(2)}) collective-permute-start(bf16[256,1024]{1,0:T(8,128)(2,1)} %get-tuple-element.220), channel_id=1, source_target_pairs={{0,4},{4,0},{8,12},{12,8},{16,20},{20,16},{24,28},{28,24},{1,5},{5... | collective-permute-start | bytes 1572872 | tf_op jit(solution)/shard_map/ppermute | solution.py:380
  180.2 9.8 %copy-start.6 = (bf16[256,1024]{1,0:T(8,128)(2,1)S(1)}, bf16[256,1024]{1,0:T(8,128)(2,1)}, u32[]{:S(2)}) copy-start(bf16[256,1024]{1,0:T(8,128)(2,1)} %get-tuple-element.226) | copy-start | bytes 1572868
  180.2 11.8 %collective-permute-start.14 = (bf16[512,1024]{1,0:T(8,128)(2,1)S(1)}, bf16[512,1024]{1,0:T(8,128)(2,1)S(1)}, u32[]{:S(2)}, u32[]{:S(2)}) collective-permute-start(bf16[512,1024]{1,0:T(8,128)(2,1)S(1)} %add_convert_fusion.1), channel_id=1, source_target_pairs={{0,1},{1,0},{2,3},{3,2},{4,5},{5,4},{6,7},{7,6},{8,9},{9,8},{10,11... | collective-permute-start | bytes 3145736 | tf_op jit(solution)/shard_map/ppermute | solution.py:380
  188.3 15.4 %collective-permute-start.17 = (bf16[256,1024]{1,0:T(8,128)(2,1)}, bf16[256,1024]{1,0:T(8,128)(2,1)S(1)}, u32[]{:S(2)}, u32[]{:S(2)}) collective-permute-start(bf16[256,1024]{1,0:T(8,128)(2,1)} %get-tuple-element.222), channel_id=1, source_target_pairs={{0,4},{4,0},{8,12},{12,8},{16,20},{20,16},{24,28},{28,24},{1,5},{5... | collective-permute-start | bytes 1572872 | tf_op jit(solution)/shard_map/ppermute | solution.py:380
  190.5 3.9 %collective-permute-start.18 = (bf16[512,1024]{1,0:T(8,128)(2,1)S(1)}, bf16[512,1024]{1,0:T(8,128)(2,1)S(1)}, u32[]{:S(2)}, u32[]{:S(2)}) collective-permute-start(bf16[512,1024]{1,0:T(8,128)(2,1)S(1)} %add_convert_fusion), channel_id=1, source_target_pairs={{0,1},{1,0},{2,3},{3,2},{4,5},{5,4},{6,7},{7,6},{8,9},{9,8},{10,11... | collective-permute-start | bytes 3145736 | tf_op jit(solution)/shard_map/ppermute | solution.py:380
  192.4 14.4 %collective-permute-start.15 = (bf16[256,1024]{1,0:T(8,128)(2,1)S(1)}, bf16[256,1024]{1,0:T(8,128)(2,1)S(1)}, u32[]{:S(2)}, u32[]{:S(2)}) collective-permute-start(bf16[256,1024]{1,0:T(8,128)(2,1)S(1)} %get-tuple-element.246), channel_id=1, source_target_pairs={{0,2},{1,3},{2,0},{3,1},{4,6},{5,7},{6,4},{7,5},{8,10},{9,11},{10,... | collective-permute-start | bytes 1572872 | tf_op jit(solution)/shard_map/ppermute | solution.py:380
  194.8 8.9 %copy-start.10 = (bf16[256,1024]{1,0:T(8,128)(2,1)S(1)}, bf16[256,1024]{1,0:T(8,128)(2,1)}, u32[]{:S(2)}) copy-start(bf16[256,1024]{1,0:T(8,128)(2,1)} %get-tuple-element.223) | copy-start | bytes 1572868
  203.6 8.0 %collective-permute-start.20 = (bf16[2,25,1024]{2,1,0:T(8,128)(2,1)S(1)}, bf16[2,25,1024]{2,1,0:T(8,128)(2,1)S(1)}, u32[]{:S(2)}, u32[]{:S(2)}) collective-permute-start(bf16[2,25,1024]{2,1,0:T(8,128)(2,1)S(1)} %convert_element_type.68), channel_id=1, source_target_pairs={{0,4},{4,0},{8,12},{12,8},{16,20},{20,16},{24,28},{28,24},{1,5},{5... | collective-permute-start | bytes 307208 | tf_op jit(solution)/shard_map/ppermute | solution.py:380
  204.9 14.8 %collective-permute-start.19 = (bf16[256,1024]{1,0:T(8,128)(2,1)S(1)}, bf16[256,1024]{1,0:T(8,128)(2,1)S(1)}, u32[]{:S(2)}, u32[]{:S(2)}) collective-permute-start(bf16[256,1024]{1,0:T(8,128)(2,1)S(1)} %get-tuple-element.232), channel_id=1, source_target_pairs={{0,2},{1,3},{2,0},{3,1},{4,6},{5,7},{6,4},{7,5},{8,10},{9,11},{10,... | collective-permute-start | bytes 1572872 | tf_op jit(solution)/shard_map/ppermute | solution.py:380
  212.6 1.4 collective-permute-start.21
  214.0 7.7 %collective-permute-start.22 = (bf16[2,25,1024]{2,1,0:T(8,128)(2,1)S(1)}, bf16[2,25,1024]{2,1,0:T(8,128)(2,1)S(1)}, u32[]{:S(2)}, u32[]{:S(2)}) collective-permute-start(bf16[2,25,1024]{2,1,0:T(8,128)(2,1)S(1)} %add_convert_fusion.4), channel_id=1, source_target_pairs={{0,2},{1,3},{2,0},{3,1},{4,6},{5,7},{6,4},{7,5},{8,10},{9,11},{10,... | collective-permute-start | bytes 307208 | tf_op jit(solution)/shard_map/ppermute | solution.py:380
  (6 other events, 8.8 us)

commit v2 on v1

--- a/solution.py
+++ b/solution.py
@@ -52,7 +52,7 @@
             lax.fori_loop(0, side, row, 0, unroll=16)
             return carry
 
-        lax.fori_loop(0, source.shape[2] // LANES, lane, 0)
+        lax.fori_loop(0, source.shape[2] // LANES, lane, 0, unroll=2)
 
     for which in range(3):
         pl.when(kind == which)(functools.partial(run, KEPT[which]))
@@ -232,14 +232,15 @@
     conv(source, lambda tap, lanes: k[0, tap, lanes][None], scalars[1 + slot], emit)
 
 
-def rest_kernel(scalars, start, *refs, slot, side, parts, mixes):
+def rest_kernel(scalars, start_in, *refs, slot, side, parts, mixes):
     if mixes:
         k, *refs = refs
     blocks = refs[:parts]
-    panel, came = refs[-2:]
+    start, panel, came = refs[-3:]
     hidden, slope = refs[parts : parts + 2]
     width = blocks[0].shape[1]
     copies = [pltpu.make_async_copy(blocks[part].at[0], panel.at[part], came.at[part]) for part in range(parts)]
+    copies.append(pltpu.make_async_copy(start_in, start, came.at[parts]))
     for copy in copies:
         copy.start()
     if mixes:
@@ -295,11 +296,15 @@
     outs = 3 if mixes else 2
     return pl.pallas_call(
         functools.partial(rest_kernel, slot=slot, side=side, parts=parts, mixes=mixes),
-        in_specs=[SMEM, VMEM] + [VMEM] * mixes + [pl.BlockSpec(memory_space=pl.ANY)] * parts,
+        in_specs=[SMEM, pl.BlockSpec(memory_space=pl.ANY)] + [VMEM] * mixes + [pl.BlockSpec(memory_space=pl.ANY)] * parts,
         out_specs=[VMEM] * outs,
         out_shape=[jax.ShapeDtypeStruct((rows, channels), jnp.bfloat16)] * outs,
         scratch_shapes=([pltpu.VMEM((side + 4, side, channels), jnp.float32)] if mixes else [])
-        + [pltpu.VMEM((parts, channels // parts, channels), jnp.bfloat16), pltpu.SemaphoreType.DMA((parts,))],
+        + [
+            pltpu.VMEM((rows, channels), jnp.bfloat16),
+            pltpu.VMEM((parts, channels // parts, channels), jnp.bfloat16),
+            pltpu.SemaphoreType.DMA((parts + 1,)),
+        ],
         compiler_params=pltpu.CompilerParams(vmem_limit_bytes=58 * MIB),
         cost_estimate=pl.CostEstimate(flops=1, bytes_accessed=1, transcendentals=0),
     )(scalars, start, *([k] if mixes else []), *blocks)

time: 225 us -> 221 us (0.982)
  Pallas kernels: 63.4 us -> 56.2 us
  waiting for transfers between devices: 119 us -> 122 us
    pallas_call x2, Pallas kernels: 12.7 us -> 9.77 us  [tap_sums(): pl.pallas_call(functools.partial(taps_kernel, slot=slot, side=side), in_s...]
    ppermute x20, waiting for transfers between devices: 49.7 us -> 52.5 us  [swap(): lax.ppermute(value, axis, [(source, source ^ bit) for source in range(cou...]
    pallas_call x5, Pallas kernels: 21.7 us -> 19.1 us  [chain(): pl.pallas_call(functools.partial(chain_kernel, pair=pair, visits=visits,...]
  transfers between devices with their start and end apart: 23 -> 23, of which waited for: 11 -> 12; matrix products, arithmetic and copies ran while one was open for 6% -> 6% of each run, Pallas kernels for 20% -> 18%
where the time goes in v2:
time: 221 us; the launch traced here: 218 us
  waiting for transfers between devices  122 us (55%)
  Pallas kernels  56.2 us (25%)
  starting transfers between devices  21.3 us (10%)
  local copies, waits for them, and re-layouts  10 us (5%)
  other arithmetic  3.97 us (2%)
  matrix products  3.66 us (2%)
    ppermute x3, waiting for transfers between devices, body(): lax.ppermute(leaving, 'segment', [(2 * source + h, 2 * source - 2 + h) fo...  69.1 us
    ppermute x20, waiting for transfers between devices, swap(): lax.ppermute(value, axis, [(source, source ^ bit) for source in range(cou...  52.5 us
    pallas_call x5, Pallas kernels, chain(): pl.pallas_call(functools.partial(chain_kernel, pair=pair, visits=visits,...  19.1 us
    ppermute x20, starting transfers between devices, swap(): lax.ppermute(value, axis, [(source, source ^ bit) for source in range(cou...  17.7 us
    pallas_call x3, Pallas kernels, forward_rest(): pl.pallas_call(functools.partial(rest_kernel, slot=slot, side=side, parts...  17 us
    pallas_call x2, Pallas kernels, tap_sums(): pl.pallas_call(functools.partial(taps_kernel, slot=slot, side=side), in_s...  9.77 us
    pallas_call x3, Pallas kernels, forward_start(): pl.pallas_call(functools.partial(start_kernel, slot=slot, side=side), in_...  8.46 us
  transfers between devices with their start and end apart: 23, of which 12 were waited for; matrix products, arithmetic and copies ran while one was open for 6% of the time, Pallas kernels for 18%

profile of v2, /device:TPU:0, one launch (start us, length us, event | category | flops | bytes accessed | tf_op | source)
XLA Modules:
  0.0 218.5 jit_solution(2379516723545191475)
XLA Ops:
  0.6 1.6 copy.52
  2.2 3.0 %collective-permute-start.5 = (bf16[2,256,1024]{2,1,0:T(8,128)(2,1)S(1)}, bf16[2,256,1024]{2,1,0:T(8,128)(2,1)S(1)}, u32[]{:S(2)}, u32[]{:S(2)}) collective-permute-start(bf16[2,256,1024]{2,1,0:T(8,128)(2,1)S(1)} %bitcast.53), channel_id=1, source_target_pairs={{0,2},{1,3},{2,0},{3,1},{4,6},{5,7},{6,4},{7,5},{8,10},{9,11},{10,... | collective-permute-start | bytes 3145736 | tf_op jit(solution)/shard_map/ppermute | solution.py:385
  5.3 1.5 collective-permute-start
  7.3 21.1 %collective-permute-done.5.refs_3_.refs_9_ = bf16[2,256,1024]{2,1,0:T(8,128)(2,1)S(1)} collective-permute-done((bf16[2,256,1024]{2,1,0:T(8,128)(2,1)S(1)}, bf16[2,256,1024]{2,1,0:T(8,128)(2,1)S(1)}, u32[]{:S(2)}, u32[]{:S(2)}) %collective-permute-start.5) | collective-permute-done | bytes 1048608 | tf_op jit(solution)/shard_map/ppermute | solution.py:385
  28.4 2.6 %dynamic-slice_bitcast_fusion = (bf16[256,1024]{1,0:T(8,128)(2,1)}, bf16[256,1024]{1,0:T(8,128)(2,1)}) fusion(bf16[2,256,1024]{2,1,0:T(8,128)(2,1)} %bitcast.79, s32[]{:T(128)S(6)} %select_n.88, s32[]{:T(128)S(6)} %select_n.86), kind=kLoop, calls=%fused_computation.12 | loop fusion | bytes 2097160 | tf_op jit(solution)/shard_map/jit(dynamic_index_in_dim)/squeeze | solution.py:432
  31.2 1.8 collective-permute-start.7
  33.0 1.5 collective-permute-start.2
  36.4 2.8 %shard_map.76.start_in = bf16[256,1024]{1,0:T(8,128)(2,1)} custom-call(s32[5]{0:T(128)} %stack.35.scalars, bf16[256,1024]{1,0:T(8,128)(2,1)} %get-tuple-element.248.x.refs_1_, f32[2,25,1024]{2,1,0:T(8,128)} %bitcast.66), custom_call_target="tpu_custom_call" | custom-call | flops 1 | bytes 1 | tf_op jit(solution)/shard_map/pallas_call | solution.py:282
  41.3 6.1 %shard_map.77 = (bf16[256,1024]{1,0:T(8,128)(2,1)}, bf16[256,1024]{1,0:T(8,128)(2,1)}, bf16[256,1024]{1,0:T(8,128)(2,1)}) custom-call(s32[5]{0:T(128)} %stack.35.scalars, bf16[256,1024]{1,0:T(8,128)(2,1)} %shard_map.76.start_in, f32[2,25,1024]{2,1,0:T(8,128)} %bitcast.67, bf16[2,256,1024]{2,1,0:T(8,128)(2,1)} %bitcast.56, ...), custom_call_target="tpu_custom_call" | custom-call | flops 1 | bytes 1 | tf_op jit(solution)/shard_map/pallas_call | solution.py:297
  47.4 5.2 %collective-permute-done.3.k.refs_6_ = f32[2,25,1024]{2,1,0:T(8,128)} collective-permute-done((f32[2,25,1024]{2,1,0:T(8,128)S(1)}, f32[2,25,1024]{2,1,0:T(8,128)}, u32[]{:S(2)}, u32[]{:S(2)}) %collective-permute-start.3) | collective-permute-done | bytes 204832 | tf_op jit(solution)/shard_map/ppermute | solution.py:385
  52.6 2.8 %shard_map.78.start_in = bf16[256,1024]{1,0:T(8,128)(2,1)} custom-call(s32[5]{0:T(128)} %stack.36.scalars, bf16[256,1024]{1,0:T(8,128)(2,1)} %collective-permute-done.2.x.refs_2_, f32[2,25,1024]{2,1,0:T(8,128)} %collective-permute-done.3.k.refs_6_), custom_call_target="tpu_custom_call" | custom-call | flops 1 | bytes 1 | tf_op jit(solution)/shard_map/pallas_call | solution.py:282
  57.3 2.4 %collective-permute-done.8.refs_1_.refs_12_ = bf16[2,256,1024]{2,1,0:T(8,128)(2,1)S(1)} collective-permute-done((bf16[2,256,1024]{2,1,0:T(8,128)(2,1)}, bf16[2,256,1024]{2,1,0:T(8,128)(2,1)S(1)}, u32[]{:S(2)}, u32[]{:S(2)}) %collective-permute-start.8) | collective-permute-done | bytes 1048608 | tf_op jit(solution)/shard_map/ppermute | solution.py:385
  59.6 1.5 collective-permute-done.9.refs_3_.refs_14_
  62.1 4.8 %shard_map.79 = (bf16[256,1024]{1,0:T(8,128)(2,1)}, bf16[256,1024]{1,0:T(8,128)(2,1)}) custom-call(s32[5]{0:T(128)} %stack.36.scalars, bf16[256,1024]{1,0:T(8,128)(2,1)} %shard_map.78.start_in, bf16[2,256,1024]{2,1,0:T(8,128)(2,1)} %collective-permute-done.refs_0_.refs_11_, bf16[2,256,1024]{2,1,0:T(8,128)(2,1)} %copy-done.8, ...), custom_call_target="tpu_custom_call" | custom-call | flops 1 | bytes 1 | tf_op jit(solution)/shard_map/pallas_call | solution.py:297
  68.1 1.6 collective-permute-start.10
  69.9 2.8 %shard_map.81.start_in = bf16[256,1024]{1,0:T(8,128)(2,1)} custom-call(s32[5]{0:T(128)} %stack.35.scalars, bf16[256,1024]{1,0:T(8,128)(2,1)} %get-tuple-element.157.x, f32[2,25,1024]{2,1,0:T(8,128)} %bitcast.69), custom_call_target="tpu_custom_call" | custom-call | flops 1 | bytes 1 | tf_op jit(solution)/shard_map/pallas_call | solution.py:282
  72.8 6.1 %shard_map.82 = (bf16[256,1024]{1,0:T(8,128)(2,1)}, bf16[256,1024]{1,0:T(8,128)(2,1)}, bf16[256,1024]{1,0:T(8,128)(2,1)}) custom-call(s32[5]{0:T(128)} %stack.35.scalars, bf16[256,1024]{1,0:T(8,128)(2,1)} %shard_map.81.start_in, f32[2,25,1024]{2,1,0:T(8,128)} %bitcast.70, bf16[2,256,1024]{2,1,0:T(8,128)(2,1)} %bitcast.58, ...), custom_call_target="tpu_custom_call" | custom-call | flops 1 | bytes 1 | tf_op jit(solution)/shard_map/pallas_call | solution.py:297
  78.9 1.3 shard_map.83
  84.4 69.0 %collective-permute-done.12.refs_0_ = bf16[256,1024]{1,0:T(8,128)(2,1)} collective-permute-done((bf16[256,1024]{1,0:T(8,128)(2,1)}, bf16[256,1024]{1,0:T(8,128)(2,1)}, u32[]{:S(2)}, u32[]{:S(2)}) %collective-permute-start.12) | collective-permute-done | bytes 524320 | tf_op jit(solution)/shard_map/ppermute | solution.py:476
  153.4 7.9 %shard_map.85 = (bf16[256,1024]{1,0:T(8,128)(2,1)}, bf16[256,1024]{1,0:T(8,128)(2,1)}, bf16[256,1024]{1,0:T(8,128)(2,1)}, bf16[256,1024]{1,0:T(8,128)(2,1)}, bf1...) custom-call(s32[5]{0:T(128)} %stack.36.scalars, ...), custom_call_target="tpu_custom_call", output_to_operand_aliasing={{0}: (16, {}), {1}: (17, {}), {2}: (18, {}), {3}: (19, {}),... | custom-call | flops 10000000000 | bytes 12582912 | tf_op jit(solution)/shard_map/pallas_call | solution.py:203
  161.3 1.5 collective-permute-start.13
  162.8 7.8 %shard_map.86 = (bf16[256,1024]{1,0:T(8,128)(2,1)}, bf16[256,1024]{1,0:T(8,128)(2,1)}, bf16[256,1024]{1,0:T(8,128)(2,1)}, bf16[256,1024]{1,0:T(8,128)(2,1)}, bf1...) custom-call(s32[5]{0:T(128)} %stack.36.scalars, ...), custom_call_target="tpu_custom_call", output_to_operand_aliasing={{0}: (16, {}), {1}: (17, {}), {2}: (18, {}), {3}: (19, {}),... | custom-call | flops 10000000000 | bytes 12582912 | tf_op jit(solution)/shard_map/pallas_call | solution.py:203
  171.2 4.8 %collective-permute-done.13 = bf16[256,1024]{1,0:T(8,128)(2,1)S(1)} collective-permute-done((bf16[256,1024]{1,0:T(8,128)(2,1)}, bf16[256,1024]{1,0:T(8,128)(2,1)S(1)}, u32[]{:S(2)}, u32[]{:S(2)}) %collective-permute-start.13) | collective-permute-done | bytes 524320 | tf_op jit(solution)/shard_map/ppermute | solution.py:385
  177.0 8.0 %collective-permute-done.16 = bf16[256,1024]{1,0:T(8,128)(2,1)S(1)} collective-permute-done((bf16[256,1024]{1,0:T(8,128)(2,1)}, bf16[256,1024]{1,0:T(8,128)(2,1)S(1)}, u32[]{:S(2)}, u32[]{:S(2)}) %collective-permute-start.16) | collective-permute-done | bytes 524320 | tf_op jit(solution)/shard_map/ppermute | solution.py:385
  185.0 1.4 collective-permute-start.17
  189.2 1.8 collective-permute-start.15
  191.8 4.9 %shard_map.89 = f32[2,25,1024]{2,1,0:T(8,128)} custom-call(s32[5]{0:T(128)} %stack.36.scalars, bf16[256,1024]{1,0:T(8,128)(2,1)} %collective-permute-done.2.x.refs_2_, bf16[256,1024]{1,0:T(8,128)(2,1)} %get-tuple-element.238.lin, bf16[256,1024]{1,0:T(8,128)(2,1)} %get-tuple-element.239.hidden, bf16[256,1024]{1,0:T(8,128)(2,1)} %get-tuple-element.240.mix), custom_call_target="tpu_custom_call" | custom-call | flops 1 | bytes 1 | tf_op jit(solution)/shard_map/pallas_call | solution.py:355
  199.8 4.1 %collective-permute-done.15.second_came = bf16[256,1024]{1,0:T(8,128)(2,1)S(1)} collective-permute-done((bf16[256,1024]{1,0:T(8,128)(2,1)S(1)}, bf16[256,1024]{1,0:T(8,128)(2,1)S(1)}, u32[]{:S(2)}, u32[]{:S(2)}) %collective-permute-start.15) | collective-permute-done | bytes 524320 | tf_op jit(solution)/shard_map/ppermute | solution.py:385
  204.0 4.9 %shard_map.88 = f32[2,25,1024]{2,1,0:T(8,128)} custom-call(s32[5]{0:T(128)} %stack.36.scalars, bf16[256,1024]{1,0:T(8,128)(2,1)} %get-tuple-element.248.x.refs_1_, bf16[256,1024]{1,0:T(8,128)(2,1)} %get-tuple-element.235.lin, bf16[256,1024]{1,0:T(8,128)(2,1)} %get-tuple-element.236.hidden, bf16[256,1024]{1,0:T(8,128)(2,1)} %get-tuple-element.237.mix), custom_call_target="tpu_custom_call" | custom-call | flops 1 | bytes 1 | tf_op jit(solution)/shard_map/pallas_call | solution.py:355
  211.3 1.8 collective-permute-start.22
  213.0 2.2 collective-permute-done.19.first_came
  215.2 1.9 shard_map.87
  (89 shorter events, 24.2 us)
Async XLA Ops:
  0.6 38.6 %copy-start = (bf16[2,1,16,16,1024]{4,3,2,1,0:T(8,128)(2,1)S(1)}, bf16[2,1,16,16,1024]{4,3,2,1,0:T(8,128)(2,1)}, u32[]{:S(2)}) copy-start(bf16[2,1,16,16,1024]{4,3,2,1,0:T(8,128)(2,1)} %param.6) | copy-start | bytes 3145732
  2.2 37.8 %copy-start.1 = (bf16[1,256,2,1024]{3,1,2,0:T(8,128)(2,1)}, bf16[1,256,2,1024]{3,1,2,0:T(8,128)(2,1)S(1)}, u32[]{:S(2)}) copy-start(bf16[1,256,2,1024]{3,1,2,0:T(8,128)(2,1)S(1)} %copy.52) | copy-start | bytes 3145732
  2.2 26.2 %collective-permute-start.5 = (bf16[2,256,1024]{2,1,0:T(8,128)(2,1)S(1)}, bf16[2,256,1024]{2,1,0:T(8,128)(2,1)S(1)}, u32[]{:S(2)}, u32[]{:S(2)}) collective-permute-start(bf16[2,256,1024]{2,1,0:T(8,128)(2,1)S(1)} %bitcast.53), channel_id=1, source_target_pairs={{0,2},{1,3},{2,0},{3,1},{4,6},{5,7},{6,4},{7,5},{8,10},{9,11},{10,... | collective-permute-start | bytes 3145736 | tf_op jit(solution)/shard_map/ppermute | solution.py:385
  5.3 25.9 %collective-permute-start = (bf16[2,256,1024]{2,1,0:T(8,128)(2,1)S(1)}, bf16[2,256,1024]{2,1,0:T(8,128)(2,1)}, u32[]{:S(2)}, u32[]{:S(2)}) collective-permute-start(bf16[2,256,1024]{2,1,0:T(8,128)(2,1)S(1)} %bitcast.54), channel_id=1, source_target_pairs={{0,4},{4,0},{8,12},{12,8},{16,20},{20,16},{24,28},{28,24},{1,5},{5... | collective-permute-start | bytes 3145736 | tf_op jit(solution)/shard_map/ppermute | solution.py:385
  6.8 34.5 %collective-permute-start.4 = (bf16[2,256,1024]{2,1,0:T(8,128)(2,1)S(1)}, bf16[2,256,1024]{2,1,0:T(8,128)(2,1)}, u32[]{:S(2)}, u32[]{:S(2)}) collective-permute-start(bf16[2,256,1024]{2,1,0:T(8,128)(2,1)S(1)} %bitcast.55), channel_id=1, source_target_pairs={{0,1},{1,0},{2,3},{3,2},{4,5},{5,4},{6,7},{7,6},{8,9},{9,8},{10,11... | collective-permute-start | bytes 3145736 | tf_op jit(solution)/shard_map/ppermute | solution.py:385
  6.8 24.4 %collective-permute-start.1 = (s32[1]{0:T(128)}, s32[1]{0:T(128)}, u32[]{:S(2)}, u32[]{:S(2)}) collective-permute-start(s32[1]{0:T(128)} %param.9), channel_id=1, source_target_pairs={{0,4},{4,0},{8,12},{12,8},{16,20},{20,16},{24,28},{28,24},{1,5},{5... | collective-permute-start | bytes 20 | tf_op jit(solution)/shard_map/ppermute | solution.py:385
  7.3 23.8 %copy-start.13 = (f32[1,2,25,1024]{3,1,2,0:T(2,128)S(1)}, f32[1,2,25,1024]{3,1,2,0:T(2,128)}, u32[]{:S(2)}) copy-start(f32[1,2,25,1024]{3,1,2,0:T(2,128)} %param.7) | copy-start | bytes 614404
  28.4 11.6 %copy-start.5 = (bf16[2,256,1024]{2,1,0:T(8,128)(2,1)}, bf16[2,256,1024]{2,1,0:T(8,128)(2,1)S(1)}, u32[]{:S(2)}) copy-start(bf16[2,256,1024]{2,1,0:T(8,128)(2,1)S(1)} %collective-permute-done.5.refs_3_.refs_9_) | copy-start | bytes 3145732
  28.4 12.9 %collective-permute-start.6 = (bf16[2,256,1024]{2,1,0:T(8,128)(2,1)S(1)}, bf16[2,256,1024]{2,1,0:T(8,128)(2,1)}, u32[]{:S(2)}, u32[]{:S(2)}) collective-permute-start(bf16[2,256,1024]{2,1,0:T(8,128)(2,1)S(1)} %collective-permute-done.5.refs_3_.refs_9_), channel_id=1, source_target_pairs={{0,1},{1,0},{2,3},{3,2},{4,5},{5,4},{6,7},{7,6},{8,9},{9,8},{10,11... | collective-permute-start | bytes 3145736 | tf_op jit(solution)/shard_map/ppermute | solution.py:385
  31.2 5.2 %copy-start.2 = (f32[1,2,25,1024]{3,2,1,0:T(8,128)}, f32[1,2,25,1024]{3,2,1,0:T(8,128)S(1)}, u32[]{:S(2)}) copy-start(f32[1,2,25,1024]{3,2,1,0:T(8,128)S(1)} %copy.53) | copy-start | bytes 614404
  31.2 25.6 %collective-permute-start.7 = (bf16[2,256,1024]{2,1,0:T(8,128)(2,1)}, bf16[2,256,1024]{2,1,0:T(8,128)(2,1)}, u32[]{:S(2)}, u32[]{:S(2)}) collective-permute-start(bf16[2,256,1024]{2,1,0:T(8,128)(2,1)} %collective-permute-done.refs_0_.refs_11_), channel_id=1, source_target_pairs={{0,2},{1,3},{2,0},{3,1},{4,6},{5,7},{6,4},{7,5},{8,10},{9,11},{10,... | collective-permute-start | bytes 3145736 | tf_op jit(solution)/shard_map/ppermute | solution.py:385
  33.0 19.6 %collective-permute-start.2 = (bf16[256,1024]{1,0:T(8,128)(2,1)}, bf16[256,1024]{1,0:T(8,128)(2,1)}, u32[]{:S(2)}, u32[]{:S(2)}) collective-permute-start(bf16[256,1024]{1,0:T(8,128)(2,1)} %get-tuple-element.157.x), channel_id=1, source_target_pairs={{0,4},{4,0},{8,12},{12,8},{16,20},{20,16},{24,28},{28,24},{1,5},{5... | collective-permute-start | bytes 1572872 | tf_op jit(solution)/shard_map/ppermute | solution.py:385
  34.5 18.1 %collective-permute-start.3 = (f32[2,25,1024]{2,1,0:T(8,128)S(1)}, f32[2,25,1024]{2,1,0:T(8,128)}, u32[]{:S(2)}, u32[]{:S(2)}) collective-permute-start(f32[2,25,1024]{2,1,0:T(8,128)S(1)} %bitcast.65), channel_id=1, source_target_pairs={{0,4},{4,0},{8,12},{12,8},{16,20},{20,16},{24,28},{28,24},{1,5},{5... | collective-permute-start | bytes 614408 | tf_op jit(solution)/shard_map/ppermute | solution.py:385
  56.8 2.9 %collective-permute-start.8 = (bf16[2,256,1024]{2,1,0:T(8,128)(2,1)}, bf16[2,256,1024]{2,1,0:T(8,128)(2,1)S(1)}, u32[]{:S(2)}, u32[]{:S(2)}) collective-permute-start(bf16[2,256,1024]{2,1,0:T(8,128)(2,1)} %collective-permute-done.refs_0_.refs_11_), channel_id=1, source_target_pairs={{0,1},{1,0},{2,3},{3,2},{4,5},{5,4},{6,7},{7,6},{8,9},{9,8},{10,11... | collective-permute-start | bytes 3145736 | tf_op jit(solution)/shard_map/ppermute | solution.py:385
  56.8 4.4 %collective-permute-start.9 = (bf16[2,256,1024]{2,1,0:T(8,128)(2,1)}, bf16[2,256,1024]{2,1,0:T(8,128)(2,1)S(1)}, u32[]{:S(2)}, u32[]{:S(2)}) collective-permute-start(bf16[2,256,1024]{2,1,0:T(8,128)(2,1)} %collective-permute-done.7.refs_2_.refs_13_), channel_id=1, source_target_pairs={{0,1},{1,0},{2,3},{3,2},{4,5},{5,4},{6,7},{7,6},{8,9},{9,8},{10,11... | collective-permute-start | bytes 3145736 | tf_op jit(solution)/shard_map/ppermute | solution.py:385
  66.9 2.8 %copy-start.4 = (bf16[256,1024]{1,0:T(8,128)(2,1)S(1)}, bf16[256,1024]{1,0:T(8,128)(2,1)}, u32[]{:S(2)}) copy-start(bf16[256,1024]{1,0:T(8,128)(2,1)} %shard_map.76.start_in) | copy-start | bytes 1572868
  68.1 10.8 %collective-permute-start.10 = (bf16[256,1024]{1,0:T(8,128)(2,1)}, bf16[256,1024]{1,0:T(8,128)(2,1)}, u32[]{:S(2)}, u32[]{:S(2)}) collective-permute-start(bf16[256,1024]{1,0:T(8,128)(2,1)} %get-tuple-element.136), channel_id=1, source_target_pairs={{24,16},{28,20},{25,17},{29,21},{26,18},{30,22},{27,19},{31,23}} | collective-permute-start | bytes 1572872 | tf_op jit(solution)/shard_map/ppermute | solution.py:476
  80.2 1.0 collective-permute-start.11
  83.0 70.4 %collective-permute-start.12 = (bf16[256,1024]{1,0:T(8,128)(2,1)}, bf16[256,1024]{1,0:T(8,128)(2,1)}, u32[]{:S(2)}, u32[]{:S(2)}) collective-permute-start(bf16[256,1024]{1,0:T(8,128)(2,1)} %get-tuple-element.193), channel_id=1, source_target_pairs={{8,0},{12,4},{9,1},{13,5},{10,2},{14,6},{11,3},{15,7}} | collective-permute-start | bytes 1572872 | tf_op jit(solution)/shard_map/ppermute | solution.py:476
  161.3 14.7 %collective-permute-start.13 = (bf16[256,1024]{1,0:T(8,128)(2,1)}, bf16[256,1024]{1,0:T(8,128)(2,1)S(1)}, u32[]{:S(2)}, u32[]{:S(2)}) collective-permute-start(bf16[256,1024]{1,0:T(8,128)(2,1)} %get-tuple-element.217), channel_id=1, source_target_pairs={{0,4},{4,0},{8,12},{12,8},{16,20},{20,16},{24,28},{28,24},{1,5},{5... | collective-permute-start | bytes 1572872 | tf_op jit(solution)/shard_map/ppermute | solution.py:385
  170.6 5.9 %copy-start.7 = (bf16[256,1024]{1,0:T(8,128)(2,1)S(1)}, bf16[256,1024]{1,0:T(8,128)(2,1)}, u32[]{:S(2)}) copy-start(bf16[256,1024]{1,0:T(8,128)(2,1)} %get-tuple-element.215) | copy-start | bytes 1572868
  170.6 14.5 %collective-permute-start.16 = (bf16[256,1024]{1,0:T(8,128)(2,1)}, bf16[256,1024]{1,0:T(8,128)(2,1)S(1)}, u32[]{:S(2)}, u32[]{:S(2)}) collective-permute-start(bf16[256,1024]{1,0:T(8,128)(2,1)} %get-tuple-element.220), channel_id=1, source_target_pairs={{0,4},{4,0},{8,12},{12,8},{16,20},{20,16},{24,28},{28,24},{1,5},{5... | collective-permute-start | bytes 1572872 | tf_op jit(solution)/shard_map/ppermute | solution.py:385
  176.9 9.9 %copy-start.6 = (bf16[256,1024]{1,0:T(8,128)(2,1)S(1)}, bf16[256,1024]{1,0:T(8,128)(2,1)}, u32[]{:S(2)}) copy-start(bf16[256,1024]{1,0:T(8,128)(2,1)} %get-tuple-element.226) | copy-start | bytes 1572868
  177.0 11.9 %collective-permute-start.14 = (bf16[512,1024]{1,0:T(8,128)(2,1)S(1)}, bf16[512,1024]{1,0:T(8,128)(2,1)S(1)}, u32[]{:S(2)}, u32[]{:S(2)}) collective-permute-start(bf16[512,1024]{1,0:T(8,128)(2,1)S(1)} %add_convert_fusion.1), channel_id=1, source_target_pairs={{0,1},{1,0},{2,3},{3,2},{4,5},{5,4},{6,7},{7,6},{8,9},{9,8},{10,11... | collective-permute-start | bytes 3145736 | tf_op jit(solution)/shard_map/ppermute | solution.py:385
  185.0 13.0 %collective-permute-start.17 = (bf16[256,1024]{1,0:T(8,128)(2,1)}, bf16[256,1024]{1,0:T(8,128)(2,1)S(1)}, u32[]{:S(2)}, u32[]{:S(2)}) collective-permute-start(bf16[256,1024]{1,0:T(8,128)(2,1)} %get-tuple-element.222), channel_id=1, source_target_pairs={{0,4},{4,0},{8,12},{12,8},{16,20},{20,16},{24,28},{28,24},{1,5},{5... | collective-permute-start | bytes 1572872 | tf_op jit(solution)/shard_map/ppermute | solution.py:385
  187.4 4.1 %collective-permute-start.18 = (bf16[512,1024]{1,0:T(8,128)(2,1)S(1)}, bf16[512,1024]{1,0:T(8,128)(2,1)S(1)}, u32[]{:S(2)}, u32[]{:S(2)}) collective-permute-start(bf16[512,1024]{1,0:T(8,128)(2,1)S(1)} %add_convert_fusion), channel_id=1, source_target_pairs={{0,1},{1,0},{2,3},{3,2},{4,5},{5,4},{6,7},{7,6},{8,9},{9,8},{10,11... | collective-permute-start | bytes 3145736 | tf_op jit(solution)/shard_map/ppermute | solution.py:385
  189.2 14.8 %collective-permute-start.15 = (bf16[256,1024]{1,0:T(8,128)(2,1)S(1)}, bf16[256,1024]{1,0:T(8,128)(2,1)S(1)}, u32[]{:S(2)}, u32[]{:S(2)}) collective-permute-start(bf16[256,1024]{1,0:T(8,128)(2,1)S(1)} %get-tuple-element.246), channel_id=1, source_target_pairs={{0,2},{1,3},{2,0},{3,1},{4,6},{5,7},{6,4},{7,5},{8,10},{9,11},{10,... | collective-permute-start | bytes 1572872 | tf_op jit(solution)/shard_map/ppermute | solution.py:385
  191.8 6.3 %copy-start.10 = (bf16[256,1024]{1,0:T(8,128)(2,1)S(1)}, bf16[256,1024]{1,0:T(8,128)(2,1)}, u32[]{:S(2)}) copy-start(bf16[256,1024]{1,0:T(8,128)(2,1)} %get-tuple-element.223) | copy-start | bytes 1572868
  197.7 11.1 %collective-permute-start.20 = (bf16[2,25,1024]{2,1,0:T(8,128)(2,1)S(1)}, bf16[2,25,1024]{2,1,0:T(8,128)(2,1)S(1)}, u32[]{:S(2)}, u32[]{:S(2)}) collective-permute-start(bf16[2,25,1024]{2,1,0:T(8,128)(2,1)S(1)} %convert_element_type.68), channel_id=1, source_target_pairs={{0,4},{4,0},{8,12},{12,8},{16,20},{20,16},{24,28},{28,24},{1,5},{5... | collective-permute-start | bytes 307208 | tf_op jit(solution)/shard_map/ppermute | solution.py:385
  199.2 16.0 %collective-permute-start.19 = (bf16[256,1024]{1,0:T(8,128)(2,1)S(1)}, bf16[256,1024]{1,0:T(8,128)(2,1)S(1)}, u32[]{:S(2)}, u32[]{:S(2)}) collective-permute-start(bf16[256,1024]{1,0:T(8,128)(2,1)S(1)} %get-tuple-element.232), channel_id=1, source_target_pairs={{0,2},{1,3},{2,0},{3,1},{4,6},{5,7},{6,4},{7,5},{8,10},{9,11},{10,... | collective-permute-start | bytes 1572872 | tf_op jit(solution)/shard_map/ppermute | solution.py:385
  209.8 1.4 collective-permute-start.21
  211.3 6.4 %collective-permute-start.22 = (bf16[2,25,1024]{2,1,0:T(8,128)(2,1)S(1)}, bf16[2,25,1024]{2,1,0:T(8,128)(2,1)S(1)}, u32[]{:S(2)}, u32[]{:S(2)}) collective-permute-start(bf16[2,25,1024]{2,1,0:T(8,128)(2,1)S(1)} %add_convert_fusion.4), channel_id=1, source_target_pairs={{0,2},{1,3},{2,0},{3,1},{4,6},{5,7},{6,4},{7,5},{8,10},{9,11},{10,... | collective-permute-start | bytes 307208 | tf_op jit(solution)/shard_map/ppermute | solution.py:385
  (6 other events, 9.2 us)
